TPU v7x, 512 devices: a whole 4x4x16 slice. The times are simulated.
512 devices in a mesh: dp: 8 (over y, x_hi), blk: 64 (over x_lo, z, core).
Axes of the slice: x: 4 (x_hi: 2, x_lo: 2; x = x_hi * 2 + x_lo), y: 4, z: 16, core: 2. Of those that a mesh axis runs over, the one named last changes fastest.
Arguments:
- gradients: bfloat16 [8, 1024, 64, 1024], P('dp', 'blk'), may hold values from -36 to 36
- left_stat: float32 [512, 128, 1024], P(('dp', 'blk')), may hold values from -300 to 3000
- right_stat: float32 [512, 128, 1024], P(('dp', 'blk')), may hold values from -300 to 3000
- left_root: bfloat16 [512, 128, 1024], P(('dp', 'blk')), may hold values from -1 to 4
- right_root: bfloat16 [512, 128, 1024], P(('dp', 'blk')), may hold values from -1 to 4
Outputs:
- update: bfloat16 [64, 1024, 1024], P('dp', None, 'blk')
- new_left: float32 [512, 128, 1024], P(('dp', 'blk'))
- new_right: float32 [512, 128, 1024], P(('dp', 'blk'))
All inputs are finite; a program needn't handle non-finite values.
Results may differ from a plain program's by a relative error of at most 0.019.
Values may be sent and summed in bfloat16 or wider, within the bound.
A program may use at most 64 MiB of HBM per device.

v0:
```python
import jax
import jax.numpy as jnp
from jax import lax
from jax.sharding import PartitionSpec as P

GROUP = 8


STAT_DECAY = 0.95
GRAFT_EPS = 1e-06


def swapped(value, axis, bit):
    mask = 2**bit
    pairs = [(source, source ^ mask) for source in range(lax.axis_size(axis))]
    return lax.ppermute(value, axis, pairs)


def place_pair(mine, partner, upper, dim):
    return jnp.where(
        upper, jnp.concatenate([partner, mine], dim), jnp.concatenate([mine, partner], dim)
    )


def on_device(gradients, left_stat, right_stat, left_root, right_root):
    replicas = lax.axis_size("dp")
    owners = lax.axis_size("blk")
    row_count = gradients.shape[1]
    block_count = gradients.shape[2]
    width = gradients.shape[3]
    slab = width // GROUP
    local_blocks = block_count // replicas
    steps_in_group = GROUP.bit_length() - 1
    arranged = gradients.reshape(row_count, replicas, owners, slab)
    exchanged = lax.all_to_all(arranged, "blk", split_axis=2, concat_axis=0, tiled=True)
    columns = lax.psum_scatter(
        exchanged.astype(jnp.float32).astype(jnp.bfloat16), "dp", scatter_dimension=1, tiled=True
    ).astype(jnp.float32)
    own_columns = columns.reshape(width, slab)
    position = lax.axis_index("blk")
    member = position % GROUP
    whole = own_columns
    right_full = right_root[0]
    for bit in range(steps_in_group):
        upper = position >> bit & 1 == 1
        partner = swapped(whole, "blk", bit)
        whole = place_pair(whole, partner, upper, 1)
    for bit in range(steps_in_group):
        upper = position >> bit & 1 == 1
        partner_rows = swapped(right_full, "blk", bit)
        right_full = place_pair(right_full, partner_rows, upper, 0)
    row_part = lax.dynamic_slice_in_dim(whole, member * slab, slab, 0)
    gram_left = jnp.einsum("rc,sc->rs", row_part, whole, precision=lax.Precision.HIGHEST)
    gram_right = jnp.einsum("rc,rd->cd", own_columns, whole, precision=lax.Precision.HIGHEST)
    new_left = (STAT_DECAY * left_stat[0] + (1.0 - STAT_DECAY) * gram_left)[None]
    new_right = (STAT_DECAY * right_stat[0] + (1.0 - STAT_DECAY) * gram_right)[None]
    summed_low = whole.astype(jnp.bfloat16)
    left_applied = jnp.dot(left_root[0], summed_low, preferred_element_type=jnp.float32).astype(
        jnp.bfloat16
    )
    preconditioned = jnp.dot(left_applied, right_full, preferred_element_type=jnp.float32)
    grad_square = jnp.sum(whole * whole)
    part_square = jnp.sum(preconditioned * preconditioned)
    update_square = part_square
    for bit in range(steps_in_group):
        update_square = update_square + swapped(update_square, "blk", bit)
    graft_scale = jnp.sqrt((grad_square + GRAFT_EPS) / (update_square + GRAFT_EPS))
    update_rows = (preconditioned * graft_scale).astype(jnp.bfloat16)
    outgoing = update_rows.reshape(1, slab, owners, width // owners)
    returned = lax.all_to_all(outgoing, "blk", split_axis=2, concat_axis=0, tiled=True)
    update = returned.reshape(local_blocks, width, width // owners)
    return (update, new_left, new_right)


def solution(mesh):
    in_specs = (
        P("dp", "blk", None, None),
        P(("dp", "blk"), None, None),
        P(("dp", "blk"), None, None),
        P(("dp", "blk"), None, None),
        P(("dp", "blk"), None, None),
    )
    out_specs = (P("dp", None, "blk"), P(("dp", "blk"), None, None), P(("dp", "blk"), None, None))
    return jax.shard_map(
        on_device, mesh=mesh, in_specs=in_specs, out_specs=out_specs, check_vma=False
    )
```

profile of v0, /device:TPU:1, one launch (start us, length us, event | category | flops | bytes accessed | tf_op | source)
XLA Modules:
  0.0 455.5 jit_solution(6267895538225064525)
XLA Ops:
  7.2 0.0 copy-start
  7.2 0.0 reduce-scatter.2.cloned.1.call-start
  7.2 2.9 reshape.26
  10.1 1.4 copy.34
  11.5 112.9 %all_to_all.33 = bf16[16,8,64,128]{3,0,1,2:T(8,128)(2,1)S(1)} all-to-all(bf16[16,8,64,128]{3,0,1,2:T(8,128)(2,1)S(1)} %copy.34), channel_id=1, replica_groups=mesh['dp'=8,'blk'=64] {'blk'}, dimensions={2} | all-to-all | bytes 4194304 | tf_op jit(solution)/shard_map/all_to_all | solution.py:35
  124.4 0.5 copy.35
  124.9 1.7 copy.36
  126.6 0.0 reduce-scatter.2.cloned.1.call-update
  126.6 86.9 %reduce-scatter.2.cloned.1.call-done = bf16[1024,1,1,128]{3,0,2,1:T(8,128)(2,1)} async-done(((bf16[1024,8,1,128]{3,0,2,1:T(8,128)(2,1)}), bf16[1024,1,1,128]{3,0,2,1:T(8,128)(2,1)}) %reduce-scatter.2.cloned.1.call-update) | async-done | bytes 262160 | tf_op jit(solution)/shard_map/reduce_scatter | solution.py:36
  213.5 1.0 bitcast_convert_fusion
  214.4 4.0 collective-permute-start
  218.5 1.5 collective-permute-done
  220.0 0.1 maximum_select_fusion.4
  220.0 3.2 collective-permute-start.1
  223.2 0.0 copy-start.5
  223.3 23.2 %collective-permute-done.1 = f32[1024,256]{1,0:T(8,128)} collective-permute-done((f32[1024,256]{1,0:T(8,128)S(1)}, f32[1024,256]{1,0:T(8,128)}, u32[]{:S(2)}, u32[]{:S(2)}) %collective-permute-start.1) | collective-permute-done | bytes 1048608 | tf_op jit(solution)/shard_map/ppermute | solution.py:16
  246.4 1.9 maximum_select_fusion.1
  248.3 4.2 collective-permute-start.2
  252.5 0.0 copy-done.5
  252.5 3.4 collective-permute-start.3
  255.9 1.1 collective-permute-done.3
  257.1 0.1 maximum_select_fusion.6
  257.2 3.2 collective-permute-start.4
  260.4 47.1 %collective-permute-done.4 = bf16[256,1024]{1,0:T(8,128)(2,1)S(1)} collective-permute-done((bf16[256,1024]{1,0:T(8,128)(2,1)S(1)}, bf16[256,1024]{1,0:T(8,128)(2,1)S(1)}, u32[]{:S(2)}, u32[]{:S(2)}) %collective-permute-start.4) | collective-permute-done | bytes 524320 | tf_op jit(solution)/shard_map/ppermute | solution.py:16
  307.5 0.5 maximum_select_fusion.5
  308.0 4.0 collective-permute-start.5
  312.1 53.1 %collective-permute-done.2 = f32[1024,512]{1,0:T(8,128)} collective-permute-done((f32[1024,512]{1,0:T(8,128)S(1)}, f32[1024,512]{1,0:T(8,128)}, u32[]{:S(2)}, u32[]{:S(2)}) %collective-permute-start.2) | collective-permute-done | bytes 2097184 | tf_op jit(solution)/shard_map/ppermute | solution.py:16
  365.1 5.2 %multiply_reduce_fusion = (f32[]{:T(128)}, f32[1024,1024]{1,0:T(8,128)}) fusion(f32[1024,512]{1,0:T(8,128)} %collective-permute-done.2, f32[1024,512]{1,0:T(8,128)S(1)} %maximum_select_fusion.1, pred[]{:T(512)S(6)} %eq.14), kind=kLoop, calls=%fused_computation.1 | loop fusion | flops 5242879 | bytes 8388613 | tf_op jit(solution)/shard_map/reduce_sum | solution.py:62
  370.3 17.3 %collective-permute-done.5 = bf16[512,1024]{1,0:T(8,128)(2,1)} collective-permute-done((bf16[512,1024]{1,0:T(8,128)(2,1)S(1)}, bf16[512,1024]{1,0:T(8,128)(2,1)}, u32[]{:S(2)}, u32[]{:S(2)}) %collective-permute-start.5) | collective-permute-done | bytes 1048608 | tf_op jit(solution)/shard_map/ppermute | solution.py:16
  387.6 0.0 copy-done
  387.6 4.9 %multiply_reduce_fusion.1 = (f32[]{:T(128)}, f32[128,1024]{1,0:T(8,128)S(1)}) fusion(bf16[512,1024]{1,0:T(8,128)(2,1)S(1)} %maximum_select_fusion.5, bf16[512,1024]{1,0:T(8,128)(2,1)} %collective-permute-done.5, pred[]{:T(512)S(6)} %eq.14, f32[1024,1024]{1,0:T(8,128)} %get-tuple-element.19, bf16[1,128,1024]{2,1,0:T(8,128)(2,1)S(1)} %copy-done), kind=kOutput, calls=%fused_computation.26 | convolution fusion | flops 547749888 | bytes 7077893 | tf_op jit(solution)/shard_map/dot_general | solution.py:61
  392.5 0.0 copy-start.3
  392.5 3.6 collective-permute-start.6
  396.7 0.3 collective-permute-done.6
  398.4 2.9 collective-permute-start.7
  401.2 1.5 collective-permute-done.7
  403.4 4.6 %collective-permute-start.8 = (f32[]{:T(128)}, f32[]{:T(128)}, u32[]{:S(2)}, u32[]{:S(2)}) collective-permute-start(f32[]{:T(128)} %add.32), channel_id=1, source_target_pairs={{0,4},{1,5},{2,6},{3,7},{4,0},{5,1},{6,2},{7,3},{8,12},{9,13},{10,... | collective-permute-start | bytes 20 | tf_op jit(solution)/shard_map/ppermute | solution.py:16
  408.0 0.7 collective-permute-done.8
  409.5 0.8 copy.37
  410.4 15.0 %all-to-all-start.1 = ((bf16[1,128,64,16]{1,3,0,2:T(8,128)(2,1)}), bf16[1,128,64,16]{1,3,0,2:T(8,128)(2,1)S(1)}, u32[]{:S(2)}, u32[]{:S(2)}) async-start(bf16[1,128,64,16]{1,3,0,2:T(8,128)(2,1)} %bitcast.7), calls=%async_computation.2 | async-start | bytes 524288 | tf_op jit(solution)/shard_map/all_to_all | solution.py:70
  425.4 0.0 copy-done.3
  425.4 0.0 copy-start.1
  425.4 0.0 copy-start.2
  425.5 0.0 copy-start.4
  425.5 7.7 %fusion.10 = f32[1,128,1024]{2,1,0:T(8,128)} fusion(f32[1024,1024]{1,0:T(8,128)} %get-tuple-element.19, s32[]{:T(128)S(6)} %select_n.68, f32[1,128,1024]{2,1,0:T(8,128)S(1)} %copy-done.3), kind=kOutput, calls=%fused_computation.15 | convolution fusion | flops 1611005952 | bytes 5767172 | tf_op jit(solution)/shard_map/rc,sc->rs/dot_general | solution.py:53
  433.2 0.0 copy-done.1
  433.2 0.0 copy-done.2
  433.2 0.0 copy-done.4
  433.2 2.4 fusion.13
  435.6 12.0 %all-to-all-done.1 = bf16[1,128,64,16]{1,3,0,2:T(8,128)(2,1)S(1)} async-done(((bf16[1,128,64,16]{1,3,0,2:T(8,128)(2,1)}), bf16[1,128,64,16]{1,3,0,2:T(8,128)(2,1)S(1)}, u32[]{:S(2)}, u32[]{:S(2)}) %all-to-all-start.1) | async-done | bytes 262176 | tf_op jit(solution)/shard_map/all_to_all | solution.py:70
  447.6 0.1 copy.39
  447.7 0.1 reshape.30
  447.8 0.9 copy.41
  (1 shorter events, 0.0 us)
Async XLA Ops:
  7.2 380.4 %copy-start = (bf16[1,128,1024]{2,1,0:T(8,128)(2,1)S(1)}, bf16[1,128,1024]{2,1,0:T(8,128)(2,1)}, u32[]{:S(2)}) copy-start(bf16[1,128,1024]{2,1,0:T(8,128)(2,1)} %param.8) | copy-start | bytes 786436
  7.2 206.3 %reduce-scatter.2.cloned.1.call-start = ((), (), s32[]{:S(2)}) async-start(), calls=%async_computation.3 | async-start | bytes 2359296 | tf_op jit(solution)/shard_map/reduce_scatter | solution.py:36
  214.4 5.5 %collective-permute-start = (f32[1024,128]{1,0:T(8,128)S(1)}, f32[1024,128]{1,0:T(8,128)S(1)}, u32[]{:S(2)}, u32[]{:S(2)}) collective-permute-start(f32[1024,128]{1,0:T(8,128)S(1)} %bitcast_convert_fusion), channel_id=1, source_target_pairs={{0,1},{1,0},{2,3},{3,2},{4,5},{5,4},{6,7},{7,6},{8,9},{9,8},{10,11... | collective-permute-start | bytes 1572872 | tf_op jit(solution)/shard_map/ppermute | solution.py:16
  220.0 26.4 %collective-permute-start.1 = (f32[1024,256]{1,0:T(8,128)S(1)}, f32[1024,256]{1,0:T(8,128)}, u32[]{:S(2)}, u32[]{:S(2)}) collective-permute-start(f32[1024,256]{1,0:T(8,128)S(1)} %maximum_select_fusion.4), channel_id=1, source_target_pairs={{0,2},{1,3},{2,0},{3,1},{4,6},{5,7},{6,4},{7,5},{8,10},{9,11},{10,... | collective-permute-start | bytes 3145736 | tf_op jit(solution)/shard_map/ppermute | solution.py:16
  223.2 29.3 %copy-start.5 = (bf16[1,128,1024]{2,1,0:T(8,128)(2,1)S(1)}, bf16[1,128,1024]{2,1,0:T(8,128)(2,1)}, u32[]{:S(2)}) copy-start(bf16[1,128,1024]{2,1,0:T(8,128)(2,1)} %param.9) | copy-start | bytes 786436
  248.3 116.8 %collective-permute-start.2 = (f32[1024,512]{1,0:T(8,128)S(1)}, f32[1024,512]{1,0:T(8,128)}, u32[]{:S(2)}, u32[]{:S(2)}) collective-permute-start(f32[1024,512]{1,0:T(8,128)S(1)} %maximum_select_fusion.1), channel_id=1, source_target_pairs={{0,4},{1,5},{2,6},{3,7},{4,0},{5,1},{6,2},{7,3},{8,12},{9,13},{10,... | collective-permute-start | bytes 6291464 | tf_op jit(solution)/shard_map/ppermute | solution.py:16
  252.5 4.5 collective-permute-start.3
  257.2 50.3 %collective-permute-start.4 = (bf16[256,1024]{1,0:T(8,128)(2,1)S(1)}, bf16[256,1024]{1,0:T(8,128)(2,1)S(1)}, u32[]{:S(2)}, u32[]{:S(2)}) collective-permute-start(bf16[256,1024]{1,0:T(8,128)(2,1)S(1)} %maximum_select_fusion.6), channel_id=1, source_target_pairs={{0,2},{1,3},{2,0},{3,1},{4,6},{5,7},{6,4},{7,5},{8,10},{9,11},{10,... | collective-permute-start | bytes 1572872 | tf_op jit(solution)/shard_map/ppermute | solution.py:16
  308.0 79.6 %collective-permute-start.5 = (bf16[512,1024]{1,0:T(8,128)(2,1)S(1)}, bf16[512,1024]{1,0:T(8,128)(2,1)}, u32[]{:S(2)}, u32[]{:S(2)}) collective-permute-start(bf16[512,1024]{1,0:T(8,128)(2,1)S(1)} %maximum_select_fusion.5), channel_id=1, source_target_pairs={{0,4},{1,5},{2,6},{3,7},{4,0},{5,1},{6,2},{7,3},{8,12},{9,13},{10,... | collective-permute-start | bytes 3145736 | tf_op jit(solution)/shard_map/ppermute | solution.py:16
  392.5 32.9 %copy-start.3 = (f32[1,128,1024]{2,1,0:T(8,128)S(1)}, f32[1,128,1024]{2,1,0:T(8,128)}, u32[]{:S(2)}) copy-start(f32[1,128,1024]{2,1,0:T(8,128)} %param.6) | copy-start | bytes 1572868
  392.5 4.5 collective-permute-start.6
  398.4 4.4 collective-permute-start.7
  403.4 5.3 %collective-permute-start.8 = (f32[]{:T(128)}, f32[]{:T(128)}, u32[]{:S(2)}, u32[]{:S(2)}) collective-permute-start(f32[]{:T(128)} %add.32), channel_id=1, source_target_pairs={{0,4},{1,5},{2,6},{3,7},{4,0},{5,1},{6,2},{7,3},{8,12},{9,13},{10,... | collective-permute-start | bytes 20 | tf_op jit(solution)/shard_map/ppermute | solution.py:16
  410.4 37.3 %all-to-all-start.1 = ((bf16[1,128,64,16]{1,3,0,2:T(8,128)(2,1)}), bf16[1,128,64,16]{1,3,0,2:T(8,128)(2,1)S(1)}, u32[]{:S(2)}, u32[]{:S(2)}) async-start(bf16[1,128,64,16]{1,3,0,2:T(8,128)(2,1)} %bitcast.7), calls=%async_computation.2 | async-start | bytes 524288 | tf_op jit(solution)/shard_map/all_to_all | solution.py:70
  425.4 7.7 %copy-start.1 = (f32[1024,1024]{1,0:T(8,128)S(1)}, f32[1024,1024]{1,0:T(8,128)}, u32[]{:S(2)}) copy-start(f32[1024,1024]{1,0:T(8,128)} %get-tuple-element.19) | copy-start | bytes 12582916
  425.4 7.7 %copy-start.2 = (bf16[1024,1,1,128]{3,0,2,1:T(8,128)(2,1)S(1)}, bf16[1024,1,1,128]{3,0,2,1:T(8,128)(2,1)}, u32[]{:S(2)}) copy-start(bf16[1024,1,1,128]{3,0,2,1:T(8,128)(2,1)} %reduce-scatter.2.cloned.1.call-done) | copy-start | bytes 786436
  425.5 7.7 %copy-start.4 = (f32[1,128,1024]{2,1,0:T(8,128)S(1)}, f32[1,128,1024]{2,1,0:T(8,128)}, u32[]{:S(2)}) copy-start(f32[1,128,1024]{2,1,0:T(8,128)} %param.7) | copy-start | bytes 1572868
Sparse Core Ops, SparseCore 0:
  126.7 86.6 reduce-scatter.1
where the time goes:
time: 456 us
  waiting for transfers between devices  245 us (54%)
  blocking collectives  113 us (25%)
  starting transfers between devices  48.1 us (11%)
  between operations  17.7 us (4%)
  matrix products  15 us (3%)
  other arithmetic  8.81 us (2%)
  local copies, waits for them, and re-layouts  8.33 us (2%)
    ppermute x9, waiting for transfers between devices, swapped(): return lax.ppermute(value, axis, pairs)  146 us
    all_to_all x1, blocking collectives, on_device(): lax.all_to_all(arranged, 'blk', split_axis=2, concat_axis=0, tiled=True)  113 us
    reduce_scatter x1, waiting for transfers between devices, on_device(): lax.psum_scatter(exchanged.astype(jnp.float32).astype(jnp.bfloat16), 'dp'...  86.9 us
    ppermute x9, starting transfers between devices, swapped(): return lax.ppermute(value, axis, pairs)  33 us
    all_to_all x1, starting transfers between devices, on_device(): lax.all_to_all(outgoing, 'blk', split_axis=2, concat_axis=0, tiled=True)  15 us
    all_to_all x1, waiting for transfers between devices, on_device(): lax.all_to_all(outgoing, 'blk', split_axis=2, concat_axis=0, tiled=True)  12 us
  transfers between devices with their start and end apart: 11, of which 11 were waited for; matrix products, arithmetic and copies ran while one was open for 4% of the time, Pallas kernels for 0%

commit v1 on v0

v1 whole, which is shorter than its diff:
```python
import functools

import jax
import jax.numpy as jnp
from jax import lax
from jax.experimental import pallas as pl
from jax.experimental.pallas import tpu as pltpu
from jax.sharding import PartitionSpec as P

GROUP = 8
STAT_DECAY = 0.95
GRAFT_EPS = 1e-06
MESH = pl.DeviceIdType.MESH
F32 = jnp.float32
BF16 = jnp.bfloat16


def remote(src, dst, send, recv, **where):
    return pltpu.make_async_remote_copy(
        src_ref=src,
        dst_ref=dst,
        send_sem=send,
        recv_sem=recv,
        device_id=where,
        device_id_type=MESH,
    )


class LineGather:
    def __init__(self, view, group, member, send, recv):
        self.view, self.group, self.member = view, group, member
        self.send, self.recv = send, recv
        self.chip, self.core = member // 2, member % 2

    def copy(self, slot, target, way):
        return remote(
            self.view(slot),
            self.view(slot),
            self.send.at[slot, way],
            self.recv.at[slot],
            blk=self.group * GROUP + target,
        )

    def to_right(self, slot):
        return self.copy(slot, self.member + 2, 0)

    def to_left(self, slot):
        return self.copy(slot, self.member - 2, 1)

    def to_sibling(self, slot):
        return self.copy(slot, self.chip * 2 + 1 - self.core, 2)

    def steps(self, act_own, act_left, act_right):
        chip, core = self.chip, self.core
        act_own(self.member)
        for hop in range(1, 4):
            pl.when(chip >= hop)(functools.partial(act_left, (chip - hop) * 2 + core))
            pl.when(chip + hop <= 3)(functools.partial(act_right, (chip + hop) * 2 + core))

    def run(self):
        chip, core = self.chip, self.core

        def own(slot):
            pl.when(chip < 3)(lambda: self.to_right(slot).start())
            pl.when(chip > 0)(lambda: self.to_left(slot).start())
            self.to_sibling(slot).start()

        def from_left(slot):
            self.to_right(slot).wait_recv()
            pl.when(chip < 3)(lambda: self.to_right(slot).start())
            self.to_sibling(slot).start()

        def from_right(slot):
            self.to_left(slot).wait_recv()
            pl.when(chip > 0)(lambda: self.to_left(slot).start())
            self.to_sibling(slot).start()

        self.steps(own, from_left, from_right)
        for other in range(4):
            self.to_sibling(other * 2 + 1 - core).wait_recv()

    def drain(self):
        chip = self.chip

        def own(slot):
            pl.when(chip < 3)(lambda: self.to_right(slot).wait_send())
            pl.when(chip > 0)(lambda: self.to_left(slot).wait_send())
            self.to_sibling(slot).wait_send()

        def from_left(slot):
            pl.when(chip < 3)(lambda: self.to_right(slot).wait_send())
            self.to_sibling(slot).wait_send()

        def from_right(slot):
            pl.when(chip > 0)(lambda: self.to_left(slot).wait_send())
            self.to_sibling(slot).wait_send()

        self.steps(own, from_left, from_right)


def kernel(
    replicas,
    owners,
    grad_ref,
    left_ref,
    right_ref,
    lroot_ref,
    rroot_ref,
    update_ref,
    newl_ref,
    newr_ref,
    land,
    fsum,
    summed,
    gbuf,
    qbuf,
    proot,
    lstat,
    rstat,
    lapp,
    uflip,
    usend,
    uland,
    squares,
    ubuf,
    local_sem,
    rs_send,
    rs_recv,
    qg_send,
    qg_recv,
    a2a_send,
    a2a_recv,
    gg_send,
    gg_recv,
    sq_send,
    sq_recv,
    up_send,
    up_recv,
    out_sem,
):
    p = lax.axis_index("dp")
    b = lax.axis_index("blk")
    groups = owners // GROUP
    group, member = b // GROUP, b % GROUP
    width = grad_ref.shape[3]
    slab = width // GROUP
    tile = 256
    tiles = width // tile

    loads = [
        pltpu.make_async_copy(grad_ref.at[:, p], land.at[0], local_sem.at[0]),
        pltpu.make_async_copy(rroot_ref, qbuf.at[member], local_sem.at[1]),
        pltpu.make_async_copy(lroot_ref, proot, local_sem.at[2]),
        pltpu.make_async_copy(left_ref, lstat, local_sem.at[3]),
        pltpu.make_async_copy(right_ref, rstat, local_sem.at[4]),
    ]
    for load in loads:
        load.start()

    barrier = pltpu.get_barrier_semaphore()
    for off in range(1, replicas):
        pl.semaphore_signal(
            barrier, inc=1, device_id={"dp": (p + off) % replicas}, device_id_type=MESH
        )

    @pl.loop(1, owners)
    def _(off):
        pl.semaphore_signal(
            barrier, inc=1, device_id={"blk": (b + off) % owners}, device_id_type=MESH
        )

    pl.semaphore_wait(barrier, replicas - 1 + owners - 1)

    def reduce_copy(off):
        to = (p + off) % replicas
        return remote(
            grad_ref.at[:, to], land.at[off], rs_send.at[off], rs_recv.at[off], dp=to
        )

    for off in range(1, replicas):
        reduce_copy(off).start()

    loads[1].wait()
    qgather = LineGather(lambda s: qbuf.at[s], group, member, qg_send, qg_recv)
    qgather.run()

    loads[0].wait()
    for off in range(1, replicas):
        reduce_copy(off).wait_recv()

    row_count = land.shape[1]

    @pl.loop(0, row_count)
    def _(row):
        total = land[0, row].astype(F32)
        for off in range(1, replicas):
            total = total + land[off, row].astype(F32)
        place = pl.ds(pl.multiple_of(row * groups, groups), groups)
        for lane in range(width // 128):
            fsum[lane, place, :] = total[:, lane * 128 : (lane + 1) * 128]

    for block in range(groups):
        for lane in range(width // 128):
            summed[block, :, lane * 128 : (lane + 1) * 128] = fsum[
                lane, pl.ds(block, row_count, stride=groups), :
            ].astype(BF16)

    def spread_copy(off):
        to = (group + off) % groups
        return remote(
            summed.at[to],
            gbuf.at[group, member],
            a2a_send.at[off],
            a2a_recv.at[off],
            blk=to * GROUP + member,
        )

    for off in range(1, groups):
        spread_copy(off).start()
    own = pltpu.make_async_copy(summed.at[group], gbuf.at[group, member], local_sem.at[5])
    own.start()
    own.wait()
    for off in range(1, groups):
        spread_copy(off).wait_recv()

    ggather = LineGather(lambda s: gbuf.at[:, s], group, member, gg_send, gg_recv)
    ggather.run()

    loads[2].wait()
    left_factor = proot[...]

    @pl.loop(0, tiles)
    def _(step):
        cols = pl.ds(pl.multiple_of(step * tile, tile), tile)
        grad = gbuf[:, :, :, cols].reshape(width, tile)
        lapp[:, cols] = jnp.dot(left_factor, grad, preferred_element_type=F32).astype(BF16)

    rows = gbuf[member].reshape(slab, width)
    wide = rows.astype(F32)
    squares[member, 0:8] = jnp.sum(
        (wide * wide).reshape(slab // 8, 8, width // 128, 128), axis=(0, 2)
    )
    squares[member, 8:16] = jnp.zeros((8, 128), F32)
    applied = lapp[...]

    @pl.loop(0, tiles)
    def _(step):
        cols = pl.ds(pl.multiple_of(step * tile, tile), tile)
        part = jnp.dot(
            applied, qbuf[:, :, cols].reshape(width, tile), preferred_element_type=F32
        )
        flip = part.T
        uflip[cols, :] = flip
        squares[member, 8:16] += jnp.sum((flip * flip).reshape(tile // 8, 8, slab), axis=0)

    def square_copy(off):
        to = (member + off) % GROUP
        return remote(
            squares.at[member],
            squares.at[member],
            sq_send.at[off],
            sq_recv.at[off],
            blk=group * GROUP + to,
        )

    for off in range(1, GROUP):
        square_copy(off).start()

    loads[3].wait()

    @pl.loop(0, tiles)
    def _(step):
        cols = pl.ds(pl.multiple_of(step * tile, tile), tile)
        per = tile // (width // groups)
        other = gbuf[pl.ds(step * per, per)].reshape(tile, width)
        gram = lax.dot_general(
            rows, other, (((1,), (1,)), ((), ())), preferred_element_type=F32
        )
        lstat[:, cols] = STAT_DECAY * lstat[:, cols] + (1.0 - STAT_DECAY) * gram

    store_left = pltpu.make_async_copy(lstat, newl_ref, out_sem.at[0])
    store_left.start()

    for off in range(1, GROUP):
        square_copy(off).wait_recv()
    total = jnp.sum(squares[...], axis=0)
    grad_square = jnp.sum(total[0:8], keepdims=True)
    update_square = jnp.sum(total[8:16], keepdims=True)
    scale = jnp.sqrt((grad_square + GRAFT_EPS) / (update_square + GRAFT_EPS))
    usend[...] = (uflip[...] * scale).astype(BF16).reshape(usend.shape)

    def update_copy(off):
        to = (b + off) % owners
        return remote(usend.at[to], uland.at[group, member], up_send, up_recv, blk=to)

    @pl.loop(1, owners)
    def _(off):
        update_copy(off).start()

    mine = pltpu.make_async_copy(usend.at[b], uland.at[group, member], up_recv)
    mine.start()

    loads[4].wait()
    first = pl.ds(pl.multiple_of(member * slab, slab), slab)
    columns = gbuf[:, :, :, first].reshape(width, slab).T

    @pl.loop(0, tiles)
    def _(step):
        cols = pl.ds(pl.multiple_of(step * tile, tile), tile)
        grad = gbuf[:, :, :, cols].reshape(width, tile)
        gram = jnp.dot(columns, grad, preferred_element_type=F32)
        rstat[:, cols] = STAT_DECAY * rstat[:, cols] + (1.0 - STAT_DECAY) * gram

    store_right = pltpu.make_async_copy(rstat, newr_ref, out_sem.at[1])
    store_right.start()

    pltpu.make_async_copy(uland, uland, up_recv).wait()
    for block in range(groups):
        for part in range(GROUP):
            ubuf[block, :, part * slab : (part + 1) * slab] = uland[block, part]
    store_update = pltpu.make_async_copy(ubuf, update_ref, out_sem.at[2])
    store_update.start()

    for off in range(1, replicas):
        reduce_copy(off).wait_send()
    qgather.drain()
    for off in range(1, groups):
        spread_copy(off).wait_send()
    ggather.drain()
    for off in range(1, GROUP):
        square_copy(off).wait_send()
    others = usend.at[pl.ds(0, owners - 1)]
    pltpu.make_async_copy(others, others, up_send).wait()
    store_left.wait()
    store_right.wait()
    store_update.wait()


def on_device(replicas, owners, gradients, left_stat, right_stat, left_root, right_root):
    _, row_count, block_count, width = gradients.shape
    local = block_count // replicas
    slab = width // GROUP
    part = width // owners
    groups = owners // GROUP
    dma = pltpu.SemaphoreType.DMA
    update, new_left, new_right = pl.pallas_call(
        functools.partial(kernel, replicas, owners),
        out_shape=(
            jax.ShapeDtypeStruct((local, part, width), BF16),
            jax.ShapeDtypeStruct((slab, width), F32),
            jax.ShapeDtypeStruct((slab, width), F32),
        ),
        in_specs=[pl.BlockSpec(memory_space=pl.ANY)] * 5,
        out_specs=[pl.BlockSpec(memory_space=pl.ANY)] * 3,
        scratch_shapes=[
            pltpu.VMEM((replicas, row_count, local, width), BF16),
            pltpu.VMEM((width // 128, row_count * local, 128), F32),
            pltpu.VMEM((local, row_count, width), BF16),
            pltpu.VMEM((groups, GROUP, row_count, width), BF16),
            pltpu.VMEM((GROUP, slab, width), BF16),
            pltpu.VMEM((slab, width), BF16),
            pltpu.VMEM((slab, width), F32),
            pltpu.VMEM((slab, width), F32),
            pltpu.VMEM((slab, width), BF16),
            pltpu.VMEM((width, slab), F32),
            pltpu.VMEM((owners, part, slab), BF16),
            pltpu.VMEM((groups, GROUP, part, slab), BF16),
            pltpu.VMEM((GROUP, 16, 128), F32),
            pltpu.VMEM((local, part, width), BF16),
            dma((6,)),
            dma((replicas,)),
            dma((replicas,)),
            dma((GROUP, 3)),
            dma((GROUP,)),
            dma((groups,)),
            dma((groups,)),
            dma((GROUP, 3)),
            dma((GROUP,)),
            dma((GROUP,)),
            dma((GROUP,)),
            dma,
            dma,
            dma((3,)),
        ],
        compiler_params=pltpu.CompilerParams(
            collective_id=0, has_side_effects=True, vmem_limit_bytes=48 * 2**20
        ),
        cost_estimate=pl.CostEstimate(
            flops=8 * slab * width * width, bytes_accessed=8 * 2**20, transcendentals=0
        ),
    )(
        gradients.reshape(row_count, replicas, local, width),
        left_stat[0],
        right_stat[0],
        left_root[0],
        right_root[0],
    )
    return jnp.swapaxes(update, 1, 2), new_left[None], new_right[None]


def solution(mesh):
    specs = (P("dp", "blk", None, None),) + (P(("dp", "blk"), None, None),) * 4
    out_specs = (P("dp", None, "blk"), P(("dp", "blk"), None, None), P(("dp", "blk"), None, None))
    return jax.shard_map(
        functools.partial(on_device, mesh.shape["dp"], mesh.shape["blk"]),
        mesh=mesh,
        in_specs=specs,
        out_specs=out_specs,
        check_vma=False,
    )
```

time: 456 us -> 114 us (0.25)
  waiting for transfers between devices: 245 us -> 0 us
  blocking collectives: 113 us -> 0 us
  Pallas kernels: 0 us -> 103 us
  starting transfers between devices: 48.1 us -> 0 us
  between operations: 17.7 us -> 0.65 us
  matrix products: 15 us -> 0 us
  other arithmetic: 8.81 us -> 0 us
    ppermute x9 -> x0, waiting for transfers between devices: 146 us -> none  [swapped(): return lax.ppermute(value, axis, pairs)]
    all_to_all x1 -> x0, blocking collectives: 113 us -> none  [on_device(): lax.all_to_all(arranged, 'blk', split_axis=2, concat_axis=0, tiled=True)]
    pallas_call x0 -> x1, Pallas kernels: none -> 103 us  [on_device(): pl.pallas_call(functools.partial(kernel, replicas, owners), out_shape=(ja...]
    reduce_scatter x1 -> x0, waiting for transfers between devices: 86.9 us -> none  [on_device(): lax.psum_scatter(exchanged.astype(jnp.float32).astype(jnp.bfloat16), 'dp'...]
    ppermute x9 -> x0, starting transfers between devices: 33 us -> none  [swapped(): return lax.ppermute(value, axis, pairs)]
    dot_general x3 -> x0, matrix products: 15 us -> none  [the longest x1 7.7 us: on_device(): jnp.einsum('rc,sc->rs', row_part, whole, precision=lax.Precision.HIGHEST)]
    all_to_all x1 -> x0, starting transfers between devices: 15 us -> none  [on_device(): lax.all_to_all(outgoing, 'blk', split_axis=2, concat_axis=0, tiled=True)]
    all_to_all x1 -> x0, waiting for transfers between devices: 12 us -> none  [on_device(): lax.all_to_all(outgoing, 'blk', split_axis=2, concat_axis=0, tiled=True)]
  transfers between devices with their start and end apart: 11 -> 0, of which waited for: 11 -> 0; matrix products, arithmetic and copies ran while one was open for 4% -> 0% of each run, Pallas kernels for 0% -> 0%
where the time goes in v1:
time: 114 us; the launch traced here: 112 us
  Pallas kernels  103 us (90%)
  local copies, waits for them, and re-layouts  7.86 us (7%)
    pallas_call x1, Pallas kernels, on_device(): pl.pallas_call(functools.partial(kernel, replicas, owners), out_shape=(ja...  103 us
    unnamed x13, local copies, waits for them, and re-layouts  7.86 us

profile of v1, /device:TPU:1, one launch (start us, length us, event | category | flops | bytes accessed | tf_op | source)
XLA Modules:
  0.0 111.9 jit_solution(2285985869643112687)
XLA Ops:
  0.6 0.0 copy-start
  0.6 1.6 %copy-done = bf16[1,16,64,1024]{3,2,1,0:T(8,128)(2,1)S(1)} copy-done((bf16[1,16,64,1024]{3,2,1,0:T(8,128)(2,1)S(1)}, bf16[1,16,64,1024]{3,2,1,0:T(8,128)(2,1)}, u32[]{:S(2)}) %copy-start) | copy-done | bytes 2097176
  2.2 0.0 copy-start.1
  2.2 1.0 copy-done.1
  3.3 0.0 copy-start.2
  3.3 1.0 copy-done.2
  4.3 0.0 copy-start.3
  4.3 0.9 copy-done.3
  5.3 0.0 copy-start.4
  5.3 0.9 copy-done.4
  6.2 103.4 %shard_map.76 = (bf16[8,16,1024]{2,1,0:T(8,128)(2,1)S(1)}, f32[128,1024]{1,0:T(8,128)S(1)}, f32[128,1024]{1,0:T(8,128)S(1)}) custom-call(bf16[16,8,8,1024]{3,2,1,0:T(8,128)(2,1)S(1)} %bitcast.11, f32[128,1024]{1,0:T(8,128)S(1)} %bitcast.12, f32[128,1024]{1,0:T(8,128)S(1)} %bitcast.13, bf16[128,1024]{1,0:T(8,128)(2,1)S(1)} %bitcast.14, ...), custom_call_target="tpu_custom_call" | custom-call | flops 1073741824 | bytes 8388608 | tf_op jit(solution)/shard_map/pallas_call | solution.py:346
  109.6 0.7 copy.11
  110.3 0.8 copy.12
  111.1 0.8 copy.13
Async XLA Ops:
  0.6 1.6 %copy-start = (bf16[1,16,64,1024]{3,2,1,0:T(8,128)(2,1)S(1)}, bf16[1,16,64,1024]{3,2,1,0:T(8,128)(2,1)}, u32[]{:S(2)}) copy-start(bf16[1,16,64,1024]{3,2,1,0:T(8,128)(2,1)} %param.5) | copy-start | bytes 6291460
  2.2 1.0 copy-start.1
  3.3 1.0 copy-start.2
  4.3 0.9 copy-start.3
  5.3 0.9 copy-start.4

commit v2 on v1

v2 whole, which is shorter than its diff:
```python
import functools

import jax
import jax.numpy as jnp
from jax import lax
from jax.experimental import pallas as pl
from jax.experimental.pallas import tpu as pltpu
from jax.sharding import PartitionSpec as P

GROUP = 8
STAT_DECAY = 0.95
GRAFT_EPS = 1e-06
MESH = pl.DeviceIdType.MESH
F32 = jnp.float32
BF16 = jnp.bfloat16


def remote(src, dst, send, recv, **where):
    return pltpu.make_async_remote_copy(
        src_ref=src,
        dst_ref=dst,
        send_sem=send,
        recv_sem=recv,
        device_id=where,
        device_id_type=MESH,
    )


class LineGather:
    def __init__(self, view, group, member, send, recv):
        self.view, self.group, self.member = view, group, member
        self.send, self.recv = send, recv
        self.chip, self.core = member // 2, member % 2

    def copy(self, slot, target, way):
        return remote(
            self.view(slot),
            self.view(slot),
            self.send.at[slot, way],
            self.recv.at[slot],
            blk=self.group * GROUP + target,
        )

    def to_right(self, slot):
        return self.copy(slot, self.member + 2, 0)

    def to_left(self, slot):
        return self.copy(slot, self.member - 2, 1)

    def to_sibling(self, slot):
        return self.copy(slot, self.chip * 2 + 1 - self.core, 2)

    def own(self):
        slot = self.member
        pl.when(self.chip < 3)(lambda: self.to_right(slot).start())
        pl.when(self.chip > 0)(lambda: self.to_left(slot).start())
        self.to_sibling(slot).start()

    def hop(self, hop):
        left, right = self.member - 2 * hop, self.member + 2 * hop

        @pl.when(self.chip >= hop)
        def _():
            self.to_right(left).wait_recv()
            pl.when(self.chip < 3)(lambda: self.to_right(left).start())
            self.to_sibling(left).start()

        @pl.when(self.chip + hop <= 3)
        def _():
            self.to_left(right).wait_recv()
            pl.when(self.chip > 0)(lambda: self.to_left(right).start())
            self.to_sibling(right).start()

    def finish(self):
        for other in range(4):
            self.to_sibling(other * 2 + 1 - self.core).wait_recv()

    def drain(self):
        chip = self.chip
        pl.when(chip < 3)(lambda: self.to_right(self.member).wait_send())
        pl.when(chip > 0)(lambda: self.to_left(self.member).wait_send())
        self.to_sibling(self.member).wait_send()
        for hop in range(1, 4):
            left, right = self.member - 2 * hop, self.member + 2 * hop

            @pl.when(chip >= hop)
            def _():
                pl.when(chip < 3)(lambda: self.to_right(left).wait_send())
                self.to_sibling(left).wait_send()

            @pl.when(chip + hop <= 3)
            def _():
                pl.when(chip > 0)(lambda: self.to_left(right).wait_send())
                self.to_sibling(right).wait_send()


def kernel(
    replicas,
    owners,
    grad_ref,
    left_ref,
    right_ref,
    lroot_ref,
    rroot_ref,
    update_ref,
    newl_ref,
    newr_ref,
    gown,
    yfar,
    ynear,
    ymix,
    yadd,
    xout,
    xpass,
    xland,
    fsum,
    summed,
    gbuf,
    qbuf,
    proot,
    lstat,
    rstat,
    lapp,
    uflip,
    usend,
    uland,
    squares,
    ubuf,
    local_sem,
    root_sem,
    y_send,
    y_recv,
    x_send,
    x_recv,
    qg_send,
    qg_recv,
    sp_send,
    gg_send,
    gg_recv,
    sib_send,
    sib_recv,
    sq_send,
    sq_recv,
    up_send,
    up_recv,
    out_sem,
):
    p = lax.axis_index("dp")
    b = lax.axis_index("blk")
    groups = owners // GROUP
    group, member = b // GROUP, b % GROUP
    chip, core = member // 2, member % 2
    y, xh = p // 2, p % 2
    xl, quarter = group // 4, group % 4
    row_count, width = grad_ref.shape[0], grad_ref.shape[3]
    half = row_count // 2
    slab = width // GROUP
    tile = 256
    tiles = width // tile

    loads = [
        pltpu.make_async_copy(grad_ref, gown, local_sem.at[0]),
        pltpu.make_async_copy(rroot_ref, qbuf.at[member], local_sem.at[1]),
        pltpu.make_async_copy(left_ref, lstat, local_sem.at[2]),
        pltpu.make_async_copy(right_ref, rstat, local_sem.at[3]),
    ]
    for block in range(GROUP):
        natural = (block // 4) * 4 + (block % 4 + quarter) % 4
        loads.append(
            pltpu.make_async_copy(
                lroot_ref.at[:, pl.ds(pl.multiple_of(natural * 128, 128), 128)],
                proot.at[:, pl.ds(block * 128, 128)],
                root_sem.at[block],
            )
        )
    loads[0].start()
    loads[1].start()

    flip = (b + owners // 2) % owners
    turn = y * 2 + 1 - xh
    near_a = {"dp": p, "blk": flip}
    near_b = {"dp": turn, "blk": flip}

    def at_y(step, which):
        return ((y + step) % 4) * 2 + which

    barrier = pltpu.get_barrier_semaphore()
    for peer in ({"dp": at_y(1, xh)}, {"dp": at_y(3, xh)}, near_b):
        pl.semaphore_signal(barrier, inc=1, device_id=peer, device_id_type=MESH)

    @pl.loop(1, owners)
    def _(off):
        pl.semaphore_signal(
            barrier, inc=1, device_id={"blk": (b + off) % owners}, device_id_type=MESH
        )

    pl.semaphore_wait(barrier, 3 + owners - 1)

    sides = (1 - xh, xh)
    steps = (1, 3)

    def rows_of(way):
        return pl.ds(way * half, half)

    def y_copy(kind, way, which):
        to = at_y(steps[way], xh)
        if kind == 0:
            src = grad_ref.at[rows_of(way), at_y(2, sides[which])]
            dst = yfar.at[way, which]
        elif kind == 1:
            src = grad_ref.at[rows_of(1 - way), at_y(steps[way], sides[which])]
            dst = ynear.at[way, which]
        else:
            src = yadd.at[way, which]
            dst = ymix.at[way, which]
        return remote(
            src, dst, y_send.at[kind, way, which], y_recv.at[kind, way, which], dp=to
        )

    def x_copy(stage, route):
        if stage == 0:
            where = (near_a, near_b)[route]
            src, dst = xout.at[route], xpass.at[route]
        else:
            where = (near_b, near_a)[route]
            src, dst = xpass.at[route], xland.at[route]
        return remote(src, dst, x_send.at[stage, route], x_recv.at[stage, route], **where)

    ways = (0, 1)
    for way in ways:
        y_copy(0, way, 0).start()
    for way in ways:
        y_copy(1, way, 0).start()
        y_copy(0, way, 1).start()

    loads[1].wait()
    qgather = LineGather(lambda s: qbuf.at[s], group, member, qg_send, qg_recv)
    qgather.own()
    for load in loads[2:]:
        load.start()
    loads[0].wait()

    for which in (0, 1):
        for way in ways:
            y_copy(0, way, which).wait_recv()

            @pl.loop(0, half)
            def _(row):
                mine = gown[way * half + row, at_y(steps[way], sides[which])]
                passed = yfar[way, which, row]
                yadd[way, which, row] = (mine.astype(F32) + passed.astype(F32)).astype(BF16)

            y_copy(2, way, which).start()
        if which == 0:
            for way in ways:
                y_copy(1, way, 1).start()
    qgather.hop(1)

    def y_total(part, which, row):
        return (
            gown[part * half + row, at_y(0, sides[which])].astype(F32)
            + ymix[part, which, row].astype(F32)
            + ynear[1 - part, which, row].astype(F32)
        )

    for part in ways:
        y_copy(2, part, 0).wait_recv()
        y_copy(1, 1 - part, 0).wait_recv()

        @pl.loop(0, half)
        def _(row):
            xout[part, row] = y_total(part, 0, row).astype(BF16)

        x_copy(0, part).start()
    for route in ways:
        x_copy(0, route).wait_recv()
        x_copy(1, route).start()
    qgather.hop(2)

    for part in ways:
        y_copy(2, part, 1).wait_recv()
        y_copy(1, 1 - part, 1).wait_recv()
        x_copy(1, part).wait_recv()

        @pl.loop(0, half)
        def _(row):
            total = y_total(part, 1, row) + xland[part, row].astype(F32)
            place = pl.ds(pl.multiple_of((part * half + row) * groups, groups), groups)
            for lane in range(width // 128):
                fsum[lane, place, :] = total[:, lane * 128 : (lane + 1) * 128]

    for block in range(groups):
        for lane in range(width // 128):
            summed[block, :, lane * 128 : (lane + 1) * 128] = fsum[
                lane, pl.ds(block, row_count, stride=groups), :
            ].astype(BF16)

    def spread_copy(across, ahead):
        to_quarter = (quarter + ahead) % 4
        to_xl = (xl + across) % 2
        slot = (chip - 4 * ahead) % 16
        if ahead == 0:
            entry = chip
        elif ahead == 1:
            entry = 0
        elif ahead == 3:
            entry = 3
        else:
            entry = jnp.where(chip <= 1, 3, 0)
        return remote(
            summed.at[to_xl * 4 + to_quarter],
            gbuf.at[xl, slot, core],
            sp_send.at[across, ahead],
            gg_recv.at[slot],
            blk=((to_xl * 4 + to_quarter) * 4 + entry) * 2 + core,
        )

    spreads = [spread_copy(across, ahead) for ahead in (2, 1, 3, 0) for across in (1, 0)]
    for spread in spreads[:-1]:
        spread.start()
    pltpu.make_async_copy(summed.at[group], gbuf.at[xl, chip, core], gg_recv.at[chip]).start()

    def pass_copy(slot, way):
        view = gbuf.at[:, slot, core]
        if way == 2:
            return remote(view, view, sib_send, sib_recv, blk=group * GROUP + chip * 2 + 1 - core)
        target = member + 2 if way == 0 else member - 2
        return remote(
            view, view, gg_send.at[way, slot], gg_recv.at[slot], blk=group * GROUP + target
        )

    def wait_slot(slot):
        view = gbuf.at[:, slot, core]
        pltpu.make_async_copy(view, view, gg_recv.at[slot]).wait()

    qgather.hop(3)

    wait_slot(chip)
    pl.when(chip < 3)(lambda: pass_copy(chip, 0).start())
    pl.when(chip > 0)(lambda: pass_copy(chip, 1).start())
    pass_copy(chip, 2).start()

    def passing(action):
        for step in range(1, 10):
            from_left = (chip - step + 16) % 16
            from_right = chip + step
            pl.when(step <= chip + 6)(functools.partial(action, from_left, 0, chip < 3))
            pl.when(step <= 9 - chip)(functools.partial(action, from_right, 1, chip > 0))

    def forward(slot, way, more):
        wait_slot(slot)
        pl.when(more)(lambda: pass_copy(slot, way).start())
        pass_copy(slot, 2).start()

    def sent(slot, way, more):
        pl.when(more)(lambda: pass_copy(slot, way).wait_send())

    passing(forward)
    qgather.finish()
    sibling = gbuf.at[:, :, 1 - core]
    pltpu.make_async_copy(sibling, sibling, sib_recv).wait()

    for load in loads[4:]:
        load.wait()
    left_factor = proot[...]

    @pl.loop(0, tiles)
    def _(step):
        cols = pl.ds(pl.multiple_of(step * tile, tile), tile)
        grad = gbuf[:, :, :, :, cols].reshape(width, tile)
        lapp[:, cols] = jnp.dot(left_factor, grad, preferred_element_type=F32).astype(BF16)

    my_rows = pl.ds((member % 4 - quarter + 4) % 4 * 4, 4)
    rows = gbuf[member // 4, my_rows].reshape(slab, width)
    wide = rows.astype(F32)
    squares[member, 0:8] = jnp.sum(
        (wide * wide).reshape(slab // 8, 8, width // 128, 128), axis=(0, 2)
    )
    squares[member, 8:16] = jnp.zeros((8, 128), F32)
    applied = lapp[...]

    @pl.loop(0, tiles)
    def _(step):
        cols = pl.ds(pl.multiple_of(step * tile, tile), tile)
        part = jnp.dot(
            applied, qbuf[:, :, cols].reshape(width, tile), preferred_element_type=F32
        )
        flipped = part.T
        uflip[cols, :] = flipped
        squares[member, 8:16] += jnp.sum(
            (flipped * flipped).reshape(tile // 8, 8, slab), axis=0
        )

    def square_copy(off):
        to = (member + off) % GROUP
        return remote(
            squares.at[member],
            squares.at[member],
            sq_send.at[off],
            sq_recv.at[off],
            blk=group * GROUP + to,
        )

    for off in range(1, GROUP):
        square_copy(off).start()

    loads[2].wait()

    @pl.loop(0, tiles)
    def _(step):
        first, slots = step // 2, pl.ds(step % 2 * 8, 8)
        other = gbuf[first, slots].reshape(tile, width)
        gram = lax.dot_general(
            rows, other, (((1,), (1,)), ((), ())), preferred_element_type=F32
        )
        for side in range(2):
            natural = first * 4 + (step % 2 * 2 + side + quarter) % 4
            cols = pl.ds(pl.multiple_of(natural * 128, 128), 128)
            lstat[:, cols] = (
                STAT_DECAY * lstat[:, cols]
                + (1.0 - STAT_DECAY) * gram[:, side * 128 : (side + 1) * 128]
            )

    store_left = pltpu.make_async_copy(lstat, newl_ref, out_sem.at[0])
    store_left.start()

    for off in range(1, GROUP):
        square_copy(off).wait_recv()
    total = jnp.sum(squares[...], axis=0)
    grad_square = jnp.sum(total[0:8], keepdims=True)
    update_square = jnp.sum(total[8:16], keepdims=True)
    scale = jnp.sqrt((grad_square + GRAFT_EPS) / (update_square + GRAFT_EPS))
    usend[...] = (uflip[...] * scale).astype(BF16).reshape(usend.shape)

    def update_copy(off):
        to = (b + off) % owners
        return remote(usend.at[to], uland.at[group, member], up_send, up_recv, blk=to)

    @pl.loop(1, owners)
    def _(off):
        update_copy(off).start()

    pltpu.make_async_copy(usend.at[b], uland.at[group, member], up_recv).start()

    loads[3].wait()
    first = pl.ds(pl.multiple_of(member * slab, slab), slab)
    columns = gbuf[:, :, :, :, first].reshape(width, slab).T

    @pl.loop(0, tiles)
    def _(step):
        cols = pl.ds(pl.multiple_of(step * tile, tile), tile)
        grad = gbuf[:, :, :, :, cols].reshape(width, tile)
        gram = jnp.dot(columns, grad, preferred_element_type=F32)
        rstat[:, cols] = STAT_DECAY * rstat[:, cols] + (1.0 - STAT_DECAY) * gram

    store_right = pltpu.make_async_copy(rstat, newr_ref, out_sem.at[1])
    store_right.start()

    for kind in range(3):
        for way in ways:
            for which in (0, 1):
                y_copy(kind, way, which).wait_send()
    for route in ways:
        x_copy(0, route).wait_send()
        x_copy(1, route).wait_send()
    qgather.drain()
    for spread in spreads[:-1]:
        spread.wait_send()
    pl.when(chip < 3)(lambda: pass_copy(chip, 0).wait_send())
    pl.when(chip > 0)(lambda: pass_copy(chip, 1).wait_send())
    passing(sent)
    lane = gbuf.at[:, :, core]
    pltpu.make_async_copy(lane, lane, sib_send).wait()
    for off in range(1, GROUP):
        square_copy(off).wait_send()

    pltpu.make_async_copy(uland, uland, up_recv).wait()
    for block in range(groups):
        for part in range(GROUP):
            ubuf[block, :, part * slab : (part + 1) * slab] = uland[block, part]
    store_update = pltpu.make_async_copy(ubuf, update_ref, out_sem.at[2])
    store_update.start()
    others = usend.at[pl.ds(0, owners - 1)]
    pltpu.make_async_copy(others, others, up_send).wait()
    store_left.wait()
    store_right.wait()
    store_update.wait()


def on_device(replicas, owners, gradients, left_stat, right_stat, left_root, right_root):
    _, row_count, block_count, width = gradients.shape
    local = block_count // replicas
    slab = width // GROUP
    part = width // owners
    groups = owners // GROUP
    dma = pltpu.SemaphoreType.DMA
    update, new_left, new_right = pl.pallas_call(
        functools.partial(kernel, replicas, owners),
        out_shape=(
            jax.ShapeDtypeStruct((local, part, width), BF16),
            jax.ShapeDtypeStruct((slab, width), F32),
            jax.ShapeDtypeStruct((slab, width), F32),
        ),
        in_specs=[pl.BlockSpec(memory_space=pl.ANY)] * 5,
        out_specs=[pl.BlockSpec(memory_space=pl.ANY)] * 3,
        scratch_shapes=[
            pltpu.VMEM((row_count, replicas, local, width), BF16),
            *[pltpu.VMEM((2, 2, row_count // 2, local, width), BF16)] * 4,
            *[pltpu.VMEM((2, row_count // 2, local, width), BF16)] * 3,
            pltpu.VMEM((width // 128, row_count * local, 128), F32),
            pltpu.VMEM((local, row_count, width), BF16),
            pltpu.VMEM((2, 16, 2, row_count, width), BF16),
            pltpu.VMEM((GROUP, slab, width), BF16),
            pltpu.VMEM((slab, width), BF16),
            pltpu.VMEM((slab, width), F32),
            pltpu.VMEM((slab, width), F32),
            pltpu.VMEM((slab, width), BF16),
            pltpu.VMEM((width, slab), F32),
            pltpu.VMEM((owners, part, slab), BF16),
            pltpu.VMEM((groups, GROUP, part, slab), BF16),
            pltpu.VMEM((GROUP, 16, 128), F32),
            pltpu.VMEM((local, part, width), BF16),
            dma((4,)),
            dma((GROUP,)),
            dma((3, 2, 2)),
            dma((3, 2, 2)),
            dma((2, 2)),
            dma((2, 2)),
            dma((GROUP, 3)),
            dma((GROUP,)),
            dma((2, 4)),
            dma((2, 16)),
            dma((16,)),
            dma,
            dma,
            dma((GROUP,)),
            dma((GROUP,)),
            dma,
            dma,
            dma((3,)),
        ],
        compiler_params=pltpu.CompilerParams(
            collective_id=0, has_side_effects=True, vmem_limit_bytes=60 * 2**20
        ),
        cost_estimate=pl.CostEstimate(
            flops=8 * slab * width * width, bytes_accessed=8 * 2**20, transcendentals=0
        ),
    )(
        gradients.reshape(row_count, replicas, local, width),
        left_stat[0],
        right_stat[0],
        left_root[0],
        right_root[0],
    )
    return jnp.swapaxes(update, 1, 2), new_left[None], new_right[None]


def solution(mesh):
    specs = (P("dp", "blk", None, None),) + (P(("dp", "blk"), None, None),) * 4
    out_specs = (P("dp", None, "blk"), P(("dp", "blk"), None, None), P(("dp", "blk"), None, None))
    return jax.shard_map(
        functools.partial(on_device, mesh.shape["dp"], mesh.shape["blk"]),
        mesh=mesh,
        in_specs=specs,
        out_specs=out_specs,
        check_vma=False,
    )
```

time: 114 us -> 109 us (0.956); the launches traced: 112 us -> 109 us
  local copies, waits for them, and re-layouts: 7.86 us -> 5.44 us
    unnamed x13 -> x3, local copies, waits for them, and re-layouts: 7.86 us -> 5.44 us
where the time goes in v2:
time: 109 us
  Pallas kernels  103 us (94%)
  local copies, waits for them, and re-layouts  5.44 us (5%)
    pallas_call x1, Pallas kernels, on_device(): pl.pallas_call(functools.partial(kernel, replicas, owners), out_shape=(ja...  103 us
    unnamed x3, local copies, waits for them, and re-layouts  5.44 us

profile of v2, /device:TPU:1, one launch (start us, length us, event | category | flops | bytes accessed | tf_op | source)
XLA Modules:
  0.0 108.7 jit_solution(850868613033186647)
XLA Ops:
  0.6 102.7 %shard_map.76 = (bf16[8,16,1024]{2,1,0:T(8,128)(2,1)}, f32[128,1024]{1,0:T(8,128)}, f32[128,1024]{1,0:T(8,128)}) custom-call(bf16[16,8,8,1024]{3,2,1,0:T(8,128)(2,1)} %bitcast.11, f32[128,1024]{1,0:T(8,128)} %bitcast.12, f32[128,1024]{1,0:T(8,128)} %bitcast.13, bf16[128,1024]{1,0:T(8,128)(2,1)} %bitcast.14, bf16[128,1024]{1,0:T(8,128)(2,1)} %bitcast.15), custom_call_target="tpu_custom_call" | custom-call | flops 1073741824 | bytes 8388608 | tf_op jit(solution)/shard_map/pallas_call | solution.py:497
  103.3 1.7 %copy.11 = bf16[8,1024,16]{1,2,0:T(8,128)(2,1)} copy(bf16[8,1024,16]{1,2,0:T(8,128)(2,1)} %bitcast.10) | data formatting | bytes 524288
  105.0 1.9 %copy.12 = f32[1,128,1024]{2,1,0:T(8,128)} copy(f32[1,128,1024]{2,1,0:T(8,128)} %bitcast.9) | data formatting | bytes 1048576
  106.9 1.9 %copy.13 = f32[1,128,1024]{2,1,0:T(8,128)} copy(f32[1,128,1024]{2,1,0:T(8,128)} %bitcast.8) | data formatting | bytes 1048576

commit v3 on v2

--- a/solution.py
+++ b/solution.py
@@ -94,17 +94,20 @@
                 self.to_sibling(right).wait_send()
 
 
-def kernel(
+def meet(peers):
+    barrier = pltpu.get_barrier_semaphore()
+    for peer in peers:
+        pl.semaphore_signal(barrier, inc=1, device_id=peer, device_id_type=MESH)
+    pl.semaphore_wait(barrier, len(peers))
+
+
+def sum_kernel(
     replicas,
     owners,
     grad_ref,
-    left_ref,
-    right_ref,
-    lroot_ref,
     rroot_ref,
-    update_ref,
-    newl_ref,
-    newr_ref,
+    summed_ref,
+    qbuf,
     gown,
     yfar,
     ynear,
@@ -115,35 +118,13 @@
     xland,
     fsum,
     summed,
-    gbuf,
-    qbuf,
-    proot,
-    lstat,
-    rstat,
-    lapp,
-    uflip,
-    usend,
-    uland,
-    squares,
-    ubuf,
     local_sem,
-    root_sem,
     y_send,
     y_recv,
     x_send,
     x_recv,
     qg_send,
     qg_recv,
-    sp_send,
-    gg_send,
-    gg_recv,
-    sib_send,
-    sib_recv,
-    sq_send,
-    sq_recv,
-    up_send,
-    up_recv,
-    out_sem,
 ):
     p = lax.axis_index("dp")
     b = lax.axis_index("blk")
@@ -154,27 +135,12 @@
     xl, quarter = group // 4, group % 4
     row_count, width = grad_ref.shape[0], grad_ref.shape[3]
     half = row_count // 2
-    slab = width // GROUP
-    tile = 256
-    tiles = width // tile
-
     loads = [
         pltpu.make_async_copy(grad_ref, gown, local_sem.at[0]),
         pltpu.make_async_copy(rroot_ref, qbuf.at[member], local_sem.at[1]),
-        pltpu.make_async_copy(left_ref, lstat, local_sem.at[2]),
-        pltpu.make_async_copy(right_ref, rstat, local_sem.at[3]),
     ]
-    for block in range(GROUP):
-        natural = (block // 4) * 4 + (block % 4 + quarter) % 4
-        loads.append(
-            pltpu.make_async_copy(
-                lroot_ref.at[:, pl.ds(pl.multiple_of(natural * 128, 128), 128)],
-                proot.at[:, pl.ds(block * 128, 128)],
-                root_sem.at[block],
-            )
-        )
-    loads[0].start()
-    loads[1].start()
+    for load in loads:
+        load.start()
 
     flip = (b + owners // 2) % owners
     turn = y * 2 + 1 - xh
@@ -184,17 +150,8 @@
     def at_y(step, which):
         return ((y + step) % 4) * 2 + which
 
-    barrier = pltpu.get_barrier_semaphore()
-    for peer in ({"dp": at_y(1, xh)}, {"dp": at_y(3, xh)}, near_b):
-        pl.semaphore_signal(barrier, inc=1, device_id=peer, device_id_type=MESH)
-
-    @pl.loop(1, owners)
-    def _(off):
-        pl.semaphore_signal(
-            barrier, inc=1, device_id={"blk": (b + off) % owners}, device_id_type=MESH
-        )
-
-    pl.semaphore_wait(barrier, 3 + owners - 1)
+    mates = [{"blk": group * GROUP + (member + off) % GROUP} for off in range(1, GROUP)]
+    meet([{"dp": at_y(1, xh)}, {"dp": at_y(3, xh)}, {"blk": flip}, near_b] + mates)
 
     sides = (1 - xh, xh)
     steps = (1, 3)
@@ -236,8 +193,6 @@
     loads[1].wait()
     qgather = LineGather(lambda s: qbuf.at[s], group, member, qg_send, qg_recv)
     qgather.own()
-    for load in loads[2:]:
-        load.start()
     loads[0].wait()
 
     for which in (0, 1):
@@ -294,6 +249,34 @@
             summed[block, :, lane * 128 : (lane + 1) * 128] = fsum[
                 lane, pl.ds(block, row_count, stride=groups), :
             ].astype(BF16)
+
+    qgather.hop(3)
+    store = pltpu.make_async_copy(summed, summed_ref, local_sem.at[2])
+    store.start()
+    qgather.finish()
+    for kind in range(3):
+        for way in ways:
+            for which in (0, 1):
+                y_copy(kind, way, which).wait_send()
+    for route in ways:
+        x_copy(0, route).wait_send()
+        x_copy(1, route).wait_send()
+    qgather.drain()
+    store.wait()
+
+
+def gather_kernel(
+    replicas, owners, summed, gbuf, sp_send, gg_send, gg_recv, sib_send, sib_recv
+):
+    p = lax.axis_index("dp")
+    b = lax.axis_index("blk")
+    groups = owners // GROUP
+    group, member = b // GROUP, b % GROUP
+    chip, core = member // 2, member % 2
+    y, xh = p // 2, p % 2
+    xl, quarter = group // 4, group % 4
+
+    meet([{"blk": (b + off) % owners} for off in range(1, owners)])
 
     def spread_copy(across, ahead):
         to_quarter = (quarter + ahead) % 4
@@ -333,8 +316,6 @@
         view = gbuf.at[:, slot, core]
         pltpu.make_async_copy(view, view, gg_recv.at[slot]).wait()
 
-    qgather.hop(3)
-
     wait_slot(chip)
     pl.when(chip < 3)(lambda: pass_copy(chip, 0).start())
     pl.when(chip > 0)(lambda: pass_copy(chip, 1).start())
@@ -356,12 +337,42 @@
         pl.when(more)(lambda: pass_copy(slot, way).wait_send())
 
     passing(forward)
-    qgather.finish()
     sibling = gbuf.at[:, :, 1 - core]
     pltpu.make_async_copy(sibling, sibling, sib_recv).wait()
-
-    for load in loads[4:]:
-        load.wait()
+    for spread in spreads[:-1]:
+        spread.wait_send()
+    pl.when(chip < 3)(lambda: pass_copy(chip, 0).wait_send())
+    pl.when(chip > 0)(lambda: pass_copy(chip, 1).wait_send())
+    passing(sent)
+    lane = gbuf.at[:, :, core]
+    pltpu.make_async_copy(lane, lane, sib_send).wait()
+
+
+def compute_kernel(
+    owners,
+    gbuf,
+    qbuf,
+    lroot_ref,
+    left_ref,
+    right_ref,
+    newl_ref,
+    newr_ref,
+    uflip,
+    squares,
+    proot,
+    lapp,
+):
+    b = lax.axis_index("blk")
+    group, member = b // GROUP, b % GROUP
+    quarter = group % 4
+    width = gbuf.shape[4]
+    slab = width // GROUP
+    tile = 256
+    tiles = width // tile
+    for block in range(GROUP):
+        natural = (block // 4) * 4 + (block % 4 + quarter) % 4
+        cols = pl.ds(pl.multiple_of(natural * 128, 128), 128)
+        proot[:, block * 128 : (block + 1) * 128] = lroot_ref[:, cols]
     left_factor = proot[...]
 
     @pl.loop(0, tiles)
@@ -373,10 +384,10 @@
     my_rows = pl.ds((member % 4 - quarter + 4) % 4 * 4, 4)
     rows = gbuf[member // 4, my_rows].reshape(slab, width)
     wide = rows.astype(F32)
-    squares[member, 0:8] = jnp.sum(
+    squares[0:8] = jnp.sum(
         (wide * wide).reshape(slab // 8, 8, width // 128, 128), axis=(0, 2)
     )
-    squares[member, 8:16] = jnp.zeros((8, 128), F32)
+    squares[8:16] = jnp.zeros((8, 128), F32)
     applied = lapp[...]
 
     @pl.loop(0, tiles)
@@ -387,9 +398,58 @@
         )
         flipped = part.T
         uflip[cols, :] = flipped
-        squares[member, 8:16] += jnp.sum(
+        squares[8:16] += jnp.sum(
             (flipped * flipped).reshape(tile // 8, 8, slab), axis=0
         )
+
+    @pl.loop(0, tiles)
+    def _(step):
+        first, slots = step // 2, pl.ds(step % 2 * 8, 8)
+        other = gbuf[first, slots].reshape(tile, width)
+        gram = lax.dot_general(
+            rows, other, (((1,), (1,)), ((), ())), preferred_element_type=F32
+        )
+        for side in range(2):
+            natural = first * 4 + (step % 2 * 2 + side + quarter) % 4
+            cols = pl.ds(pl.multiple_of(natural * 128, 128), 128)
+            newl_ref[:, cols] = (
+                STAT_DECAY * left_ref[:, cols]
+                + (1.0 - STAT_DECAY) * gram[:, side * 128 : (side + 1) * 128]
+            )
+
+    first = pl.ds(pl.multiple_of(member * slab, slab), slab)
+    columns = gbuf[:, :, :, :, first].reshape(width, slab).T
+
+    @pl.loop(0, tiles)
+    def _(step):
+        cols = pl.ds(pl.multiple_of(step * tile, tile), tile)
+        grad = gbuf[:, :, :, :, cols].reshape(width, tile)
+        gram = jnp.dot(columns, grad, preferred_element_type=F32)
+        newr_ref[:, cols] = STAT_DECAY * right_ref[:, cols] + (1.0 - STAT_DECAY) * gram
+
+
+def update_kernel(
+    owners,
+    uflip,
+    square_ref,
+    update_ref,
+    squares,
+    usend,
+    uland,
+    ubuf,
+    sq_send,
+    sq_recv,
+    up_send,
+    up_recv,
+    out_sem,
+):
+    b = lax.axis_index("blk")
+    groups = owners // GROUP
+    group, member = b // GROUP, b % GROUP
+    slab = usend.shape[2]
+    meet([{"blk": (b + off) % owners} for off in range(1, owners)])
+
+    squares[member] = square_ref[...]
 
     def square_copy(off):
         to = (member + off) % GROUP
@@ -404,26 +464,6 @@
     for off in range(1, GROUP):
         square_copy(off).start()
 
-    loads[2].wait()
-
-    @pl.loop(0, tiles)
-    def _(step):
-        first, slots = step // 2, pl.ds(step % 2 * 8, 8)
-        other = gbuf[first, slots].reshape(tile, width)
-        gram = lax.dot_general(
-            rows, other, (((1,), (1,)), ((), ())), preferred_element_type=F32
-        )
-        for side in range(2):
-            natural = first * 4 + (step % 2 * 2 + side + quarter) % 4
-            cols = pl.ds(pl.multiple_of(natural * 128, 128), 128)
-            lstat[:, cols] = (
-                STAT_DECAY * lstat[:, cols]
-                + (1.0 - STAT_DECAY) * gram[:, side * 128 : (side + 1) * 128]
-            )
-
-    store_left = pltpu.make_async_copy(lstat, newl_ref, out_sem.at[0])
-    store_left.start()
-
     for off in range(1, GROUP):
         square_copy(off).wait_recv()
     total = jnp.sum(squares[...], axis=0)
@@ -441,38 +481,6 @@
         update_copy(off).start()
 
     pltpu.make_async_copy(usend.at[b], uland.at[group, member], up_recv).start()
-
-    loads[3].wait()
-    first = pl.ds(pl.multiple_of(member * slab, slab), slab)
-    columns = gbuf[:, :, :, :, first].reshape(width, slab).T
-
-    @pl.loop(0, tiles)
-    def _(step):
-        cols = pl.ds(pl.multiple_of(step * tile, tile), tile)
-        grad = gbuf[:, :, :, :, cols].reshape(width, tile)
-        gram = jnp.dot(columns, grad, preferred_element_type=F32)
-        rstat[:, cols] = STAT_DECAY * rstat[:, cols] + (1.0 - STAT_DECAY) * gram
-
-    store_right = pltpu.make_async_copy(rstat, newr_ref, out_sem.at[1])
-    store_right.start()
-
-    for kind in range(3):
-        for way in ways:
-            for which in (0, 1):
-                y_copy(kind, way, which).wait_send()
-    for route in ways:
-        x_copy(0, route).wait_send()
-        x_copy(1, route).wait_send()
-    qgather.drain()
-    for spread in spreads[:-1]:
-        spread.wait_send()
-    pl.when(chip < 3)(lambda: pass_copy(chip, 0).wait_send())
-    pl.when(chip > 0)(lambda: pass_copy(chip, 1).wait_send())
-    passing(sent)
-    lane = gbuf.at[:, :, core]
-    pltpu.make_async_copy(lane, lane, sib_send).wait()
-    for off in range(1, GROUP):
-        square_copy(off).wait_send()
 
     pltpu.make_async_copy(uland, uland, up_recv).wait()
     for block in range(groups):
@@ -482,8 +490,8 @@
     store_update.start()
     others = usend.at[pl.ds(0, owners - 1)]
     pltpu.make_async_copy(others, others, up_send).wait()
-    store_left.wait()
-    store_right.wait()
+    for off in range(1, GROUP):
+        square_copy(off).wait_send()
     store_update.wait()
 
 
@@ -494,64 +502,81 @@
     part = width // owners
     groups = owners // GROUP
     dma = pltpu.SemaphoreType.DMA
-    update, new_left, new_right = pl.pallas_call(
-        functools.partial(kernel, replicas, owners),
+    anywhere = pl.BlockSpec(memory_space=pl.ANY)
+    vmem = pl.BlockSpec(memory_space=pltpu.VMEM)
+    struct = jax.ShapeDtypeStruct
+
+    def params(number):
+        return pltpu.CompilerParams(
+            collective_id=number, has_side_effects=True, vmem_limit_bytes=24 * 2**20
+        )
+
+    summed, right_full = pl.pallas_call(
+        functools.partial(sum_kernel, replicas, owners),
         out_shape=(
-            jax.ShapeDtypeStruct((local, part, width), BF16),
-            jax.ShapeDtypeStruct((slab, width), F32),
-            jax.ShapeDtypeStruct((slab, width), F32),
+            struct((local, row_count, width), BF16),
+            struct((GROUP, slab, width), BF16),
         ),
-        in_specs=[pl.BlockSpec(memory_space=pl.ANY)] * 5,
-        out_specs=[pl.BlockSpec(memory_space=pl.ANY)] * 3,
+        in_specs=[anywhere] * 2,
+        out_specs=[anywhere] * 2,
         scratch_shapes=[
             pltpu.VMEM((row_count, replicas, local, width), BF16),
             *[pltpu.VMEM((2, 2, row_count // 2, local, width), BF16)] * 4,
             *[pltpu.VMEM((2, row_count // 2, local, width), BF16)] * 3,
             pltpu.VMEM((width // 128, row_count * local, 128), F32),
             pltpu.VMEM((local, row_count, width), BF16),
-            pltpu.VMEM((2, 16, 2, row_count, width), BF16),
-            pltpu.VMEM((GROUP, slab, width), BF16),
-            pltpu.VMEM((slab, width), BF16),
-            pltpu.VMEM((slab, width), F32),
-            pltpu.VMEM((slab, width), F32),
-            pltpu.VMEM((slab, width), BF16),
-            pltpu.VMEM((width, slab), F32),
-            pltpu.VMEM((owners, part, slab), BF16),
-            pltpu.VMEM((groups, GROUP, part, slab), BF16),
-            pltpu.VMEM((GROUP, 16, 128), F32),
-            pltpu.VMEM((local, part, width), BF16),
-            dma((4,)),
-            dma((GROUP,)),
+            dma((3,)),
             dma((3, 2, 2)),
             dma((3, 2, 2)),
             dma((2, 2)),
             dma((2, 2)),
             dma((GROUP, 3)),
             dma((GROUP,)),
-            dma((2, 4)),
-            dma((2, 16)),
-            dma((16,)),
-            dma,
-            dma,
+        ],
+        compiler_params=params(0),
+    )(gradients.reshape(row_count, replicas, local, width), right_root[0])
+
+    whole = pl.pallas_call(
+        functools.partial(gather_kernel, replicas, owners),
+        out_shape=struct((2, 16, 2, row_count, width), BF16),
+        in_specs=[anywhere],
+        out_specs=anywhere,
+        scratch_shapes=[dma((2, 4)), dma((2, 16)), dma((16,)), dma, dma],
+        compiler_params=params(1),
+    )(summed)
+
+    new_left, new_right, uflip, square = pl.pallas_call(
+        functools.partial(compute_kernel, owners),
+        out_shape=(
+            struct((slab, width), F32),
+            struct((slab, width), F32),
+            struct((width, slab), F32),
+            struct((16, 128), F32),
+        ),
+        in_specs=[vmem] * 5,
+        out_specs=[vmem] * 4,
+        scratch_shapes=[pltpu.VMEM((slab, width), BF16)] * 2,
+        compiler_params=pltpu.CompilerParams(vmem_limit_bytes=24 * 2**20),
+    )(whole, right_full, left_root[0], left_stat[0], right_stat[0])
+
+    update = pl.pallas_call(
+        functools.partial(update_kernel, owners),
+        out_shape=struct((local, part, width), BF16),
+        in_specs=[vmem] * 2,
+        out_specs=anywhere,
+        scratch_shapes=[
+            pltpu.VMEM((GROUP, 16, 128), F32),
+            pltpu.VMEM((owners, part, slab), BF16),
+            pltpu.VMEM((groups, GROUP, part, slab), BF16),
+            pltpu.VMEM((local, part, width), BF16),
             dma((GROUP,)),
             dma((GROUP,)),
             dma,
             dma,
             dma((3,)),
         ],
-        compiler_params=pltpu.CompilerParams(
-            collective_id=0, has_side_effects=True, vmem_limit_bytes=60 * 2**20
-        ),
-        cost_estimate=pl.CostEstimate(
-            flops=8 * slab * width * width, bytes_accessed=8 * 2**20, transcendentals=0
-        ),
-    )(
-        gradients.reshape(row_count, replicas, local, width),
-        left_stat[0],
-        right_stat[0],
-        left_root[0],
-        right_root[0],
-    )
+        compiler_params=params(2),
+    )(uflip, square)
     return jnp.swapaxes(update, 1, 2), new_left[None], new_right[None]
 
 

time: 109 us -> 123 us (1.13)
  Pallas kernels: 103 us -> 119 us
  local copies, waits for them, and re-layouts: 5.44 us -> 3.25 us
    pallas_call x1 -> x4, Pallas kernels: 103 us -> 119 us  [the longest x1 51.2 us: on_device(): pl.pallas_call(functools.partial(gather_kernel, replicas, owners), out_sh...]
    unnamed x3 -> x11, local copies, waits for them, and re-layouts: 5.44 us -> 3.25 us
where the time goes in v3:
time: 123 us
  Pallas kernels  119 us (97%)
  local copies, waits for them, and re-layouts  3.25 us (3%)
    pallas_call x1, Pallas kernels, on_device(): pl.pallas_call(functools.partial(gather_kernel, replicas, owners), out_sh...  51.2 us
    pallas_call x1, Pallas kernels, on_device(): pl.pallas_call(functools.partial(sum_kernel, replicas, owners), out_shape...  36.1 us
    pallas_call x1, Pallas kernels, on_device(): pl.pallas_call(functools.partial(update_kernel, owners), out_shape=struct...  26 us
    pallas_call x1, Pallas kernels, on_device(): pl.pallas_call(functools.partial(compute_kernel, owners), out_shape=(stru...  5.82 us
    unnamed x11, local copies, waits for them, and re-layouts  3.25 us

profile of v3, /device:TPU:1, one launch (start us, length us, event | category | flops | bytes accessed | tf_op | source)
XLA Modules:
  0.0 123.1 jit_solution(9319519098297500242)
XLA Ops:
  0.6 0.0 copy-start
  0.6 1.6 %copy-done = bf16[1,16,64,1024]{3,2,1,0:T(8,128)(2,1)S(1)} copy-done((bf16[1,16,64,1024]{3,2,1,0:T(8,128)(2,1)S(1)}, bf16[1,16,64,1024]{3,2,1,0:T(8,128)(2,1)}, u32[]{:S(2)}) %copy-start) | copy-done | bytes 2097176
  2.2 0.0 copy-start.3
  2.2 0.9 copy-done.3
  3.2 0.0 copy-start.1
  3.2 0.0 copy-start.2
  3.2 0.0 copy-start.4
  3.2 36.1 %shard_map.76 = (bf16[8,16,1024]{2,1,0:T(8,128)(2,1)S(1)}, bf16[8,128,1024]{2,1,0:T(8,128)(2,1)S(1)}) custom-call(bf16[16,8,8,1024]{3,2,1,0:T(8,128)(2,1)S(1)} %bitcast.8, bf16[128,1024]{1,0:T(8,128)(2,1)S(1)} %bitcast.12), custom_call_target="tpu_custom_call" | custom-call | tf_op jit(solution)/shard_map/pallas_call | solution.py:514
  39.3 51.2 %shard_map.77.gbuf = bf16[2,16,2,16,1024]{4,3,2,1,0:T(8,128)(2,1)S(1)} custom-call(bf16[8,16,1024]{2,1,0:T(8,128)(2,1)S(1)} %get-tuple-element.9.summed), custom_call_target="tpu_custom_call" | custom-call | tf_op jit(solution)/shard_map/pallas_call | solution.py:539
  90.5 0.0 copy-done.1
  90.5 0.0 copy-done.2
  90.5 0.0 copy-done.4
  90.5 5.8 %shard_map.78 = (f32[128,1024]{1,0:T(8,128)}, f32[128,1024]{1,0:T(8,128)}, f32[1024,128]{1,0:T(8,128)S(1)}, f32[16,128]{1,0:T(8,128)S(1)}) custom-call(bf16[2,16,2,16,1024]{4,3,2,1,0:T(8,128)(2,1)S(1)} %shard_map.77.gbuf, bf16[8,128,1024]{2,1,0:T(8,128)(2,1)S(1)} %get-tuple-element.10.qbuf, bf16[128,1024]{1,0:T(8,128)(2,1)S(1)} %bitcast.13, ...), custom_call_target="tpu_custom_call" | custom-call | tf_op jit(solution)/shard_map/pallas_call | solution.py:548
  96.3 26.0 %shard_map.79 = bf16[8,16,1024]{2,1,0:T(8,128)(2,1)S(1)} custom-call(f32[1024,128]{1,0:T(8,128)S(1)} %get-tuple-element.11.uflip, f32[16,128]{1,0:T(8,128)S(1)} %get-tuple-element.12.square_ref), custom_call_target="tpu_custom_call" | custom-call | tf_op jit(solution)/shard_map/pallas_call | solution.py:562
  122.4 0.7 copy.9
Async XLA Ops:
  0.6 1.6 %copy-start = (bf16[1,16,64,1024]{3,2,1,0:T(8,128)(2,1)S(1)}, bf16[1,16,64,1024]{3,2,1,0:T(8,128)(2,1)}, u32[]{:S(2)}) copy-start(bf16[1,16,64,1024]{3,2,1,0:T(8,128)(2,1)} %param.5) | copy-start | bytes 6291460
  2.2 0.9 copy-start.3
  3.2 87.3 %copy-start.1 = (f32[1,128,1024]{2,1,0:T(8,128)S(1)}, f32[1,128,1024]{2,1,0:T(8,128)}, u32[]{:S(2)}) copy-start(f32[1,128,1024]{2,1,0:T(8,128)} %param.6) | copy-start | bytes 1572868
  3.2 87.3 %copy-start.2 = (f32[1,128,1024]{2,1,0:T(8,128)S(1)}, f32[1,128,1024]{2,1,0:T(8,128)}, u32[]{:S(2)}) copy-start(f32[1,128,1024]{2,1,0:T(8,128)} %param.7) | copy-start | bytes 1572868
  3.2 87.3 %copy-start.4 = (bf16[1,128,1024]{2,1,0:T(8,128)(2,1)S(1)}, bf16[1,128,1024]{2,1,0:T(8,128)(2,1)}, u32[]{:S(2)}) copy-start(bf16[1,128,1024]{2,1,0:T(8,128)(2,1)} %param.8) | copy-start | bytes 786436

commit v4 on v2

--- a/solution.py
+++ b/solution.py
@@ -120,11 +120,12 @@
     proot,
     lstat,
     rstat,
+    lacc,
     lapp,
-    uflip,
     usend,
     uland,
     squares,
+    scales,
     ubuf,
     local_sem,
     root_sem,
@@ -141,6 +142,8 @@
     sib_recv,
     sq_send,
     sq_recv,
+    sc_send,
+    sc_recv,
     up_send,
     up_recv,
     out_sem,
@@ -165,7 +168,7 @@
         pltpu.make_async_copy(right_ref, rstat, local_sem.at[3]),
     ]
     for block in range(GROUP):
-        natural = (block // 4) * 4 + (block % 4 + quarter) % 4
+        natural = (block % 2) * 4 + (block // 2 + quarter) % 4
         loads.append(
             pltpu.make_async_copy(
                 lroot_ref.at[:, pl.ds(pl.multiple_of(natural * 128, 128), 128)],
@@ -309,28 +312,33 @@
             entry = jnp.where(chip <= 1, 3, 0)
         return remote(
             summed.at[to_xl * 4 + to_quarter],
-            gbuf.at[xl, slot, core],
+            gbuf.at[slot // 4, xl, slot % 4, core],
             sp_send.at[across, ahead],
             gg_recv.at[slot],
             blk=((to_xl * 4 + to_quarter) * 4 + entry) * 2 + core,
         )
 
-    spreads = [spread_copy(across, ahead) for ahead in (2, 1, 3, 0) for across in (1, 0)]
-    for spread in spreads[:-1]:
+    def slot_view(slot, which=core):
+        return gbuf.at[slot // 4, :, slot % 4, which]
+
+    spreads = [spread_copy(1, 0)]
+    spreads += [spread_copy(across, ahead) for ahead in (2, 1, 3) for across in (1, 0)]
+    for spread in spreads:
         spread.start()
-    pltpu.make_async_copy(summed.at[group], gbuf.at[xl, chip, core], gg_recv.at[chip]).start()
+    own_slot = gbuf.at[0, xl, chip, core]
+    pltpu.make_async_copy(summed.at[group], own_slot, gg_recv.at[chip]).start()
 
     def pass_copy(slot, way):
-        view = gbuf.at[:, slot, core]
+        view = slot_view(slot)
         if way == 2:
-            return remote(view, view, sib_send, sib_recv, blk=group * GROUP + chip * 2 + 1 - core)
+            return remote(view, view, sib_send.at[slot], sib_recv.at[slot], blk=group * GROUP + chip * 2 + 1 - core)
         target = member + 2 if way == 0 else member - 2
         return remote(
             view, view, gg_send.at[way, slot], gg_recv.at[slot], blk=group * GROUP + target
         )
 
     def wait_slot(slot):
-        view = gbuf.at[:, slot, core]
+        view = slot_view(slot)
         pltpu.make_async_copy(view, view, gg_recv.at[slot]).wait()
 
     qgather.hop(3)
@@ -340,12 +348,14 @@
     pl.when(chip > 0)(lambda: pass_copy(chip, 1).start())
     pass_copy(chip, 2).start()
 
-    def passing(action):
+    def passing(action, between=None):
         for step in range(1, 10):
             from_left = (chip - step + 16) % 16
             from_right = chip + step
             pl.when(step <= chip + 6)(functools.partial(action, from_left, 0, chip < 3))
             pl.when(step <= 9 - chip)(functools.partial(action, from_right, 1, chip > 0))
+            if between is not None:
+                between(step)
 
     def forward(slot, way, more):
         wait_slot(slot)
@@ -355,41 +365,72 @@
     def sent(slot, way, more):
         pl.when(more)(lambda: pass_copy(slot, way).wait_send())
 
-    passing(forward)
+    def apply_quad(quad, first):
+        for slot in range(quad * 4, quad * 4 + 4):
+            view = slot_view(slot, 1 - core)
+            pltpu.make_async_copy(view, view, sib_recv.at[slot]).wait()
+        factor = proot[:, quad * 256 : (quad + 1) * 256]
+
+        @pl.loop(0, tiles)
+        def _(step):
+            cols = pl.ds(pl.multiple_of(step * tile, tile), tile)
+            grad = gbuf[quad, :, :, :, :, cols].reshape(256, tile)
+            part = jnp.dot(factor, grad, preferred_element_type=F32)
+            if not first:
+                part = part + lacc[:, cols]
+            if quad == 2:
+                lapp[:, cols] = part.astype(BF16)
+            else:
+                lacc[:, cols] = part
+
+    def compute(step):
+        if step == 4:
+            for load in loads[4:]:
+                load.wait()
+            apply_quad(0, True)
+        elif step == 7:
+            apply_quad(1, False)
+        elif step == 8:
+            apply_quad(3, False)
+
+    passing(forward, compute)
     qgather.finish()
-    sibling = gbuf.at[:, :, 1 - core]
-    pltpu.make_async_copy(sibling, sibling, sib_recv).wait()
-
-    for load in loads[4:]:
-        load.wait()
-    left_factor = proot[...]
-
-    @pl.loop(0, tiles)
-    def _(step):
-        cols = pl.ds(pl.multiple_of(step * tile, tile), tile)
-        grad = gbuf[:, :, :, :, cols].reshape(width, tile)
-        lapp[:, cols] = jnp.dot(left_factor, grad, preferred_element_type=F32).astype(BF16)
-
-    my_rows = pl.ds((member % 4 - quarter + 4) % 4 * 4, 4)
-    rows = gbuf[member // 4, my_rows].reshape(slab, width)
+    apply_quad(2, False)
+
+    applied = lapp[...]
+    squares[member] = jnp.zeros((16, 128), F32)
+    per_tile = owners // tiles
+
+    def update_copy(to):
+        return remote(usend.at[to], uland.at[group, member], up_send, up_recv, blk=to)
+
+    mine = pltpu.make_async_copy(usend.at[b], uland.at[group, member], up_recv)
+    for turn_tile in (1, 2, 3, 0):
+        number = (b // per_tile + turn_tile) % tiles
+        cols = pl.ds(pl.multiple_of(number * tile, tile), tile)
+        part = jnp.dot(
+            applied, qbuf[:, :, cols].reshape(width, tile), preferred_element_type=F32
+        )
+        flipped = part.T
+        usend[pl.ds(number * per_tile, per_tile)] = flipped.astype(BF16).reshape(
+            per_tile, tile // per_tile, slab
+        )
+        squares[member, 8:16] += jnp.sum(
+            (flipped * flipped).reshape(tile // 8, 8, slab), axis=0
+        )
+        if turn_tile == 0:
+            mine.start()
+
+        @pl.loop(1 if turn_tile == 0 else 0, per_tile)
+        def _(off):
+            update_copy(number * per_tile + (b + off) % per_tile).start()
+
+    my_quad = (member % 4 - quarter + 4) % 4
+    rows = gbuf[my_quad, member // 4].reshape(slab, width)
     wide = rows.astype(F32)
     squares[member, 0:8] = jnp.sum(
         (wide * wide).reshape(slab // 8, 8, width // 128, 128), axis=(0, 2)
     )
-    squares[member, 8:16] = jnp.zeros((8, 128), F32)
-    applied = lapp[...]
-
-    @pl.loop(0, tiles)
-    def _(step):
-        cols = pl.ds(pl.multiple_of(step * tile, tile), tile)
-        part = jnp.dot(
-            applied, qbuf[:, :, cols].reshape(width, tile), preferred_element_type=F32
-        )
-        flipped = part.T
-        uflip[cols, :] = flipped
-        squares[member, 8:16] += jnp.sum(
-            (flipped * flipped).reshape(tile // 8, 8, slab), axis=0
-        )
 
     def square_copy(off):
         to = (member + off) % GROUP
@@ -408,13 +449,12 @@
 
     @pl.loop(0, tiles)
     def _(step):
-        first, slots = step // 2, pl.ds(step % 2 * 8, 8)
-        other = gbuf[first, slots].reshape(tile, width)
+        other = gbuf[step].reshape(tile, width)
         gram = lax.dot_general(
             rows, other, (((1,), (1,)), ((), ())), preferred_element_type=F32
         )
         for side in range(2):
-            natural = first * 4 + (step % 2 * 2 + side + quarter) % 4
+            natural = side * 4 + (step + quarter) % 4
             cols = pl.ds(pl.multiple_of(natural * 128, 128), 128)
             lstat[:, cols] = (
                 STAT_DECAY * lstat[:, cols]
@@ -430,26 +470,29 @@
     grad_square = jnp.sum(total[0:8], keepdims=True)
     update_square = jnp.sum(total[8:16], keepdims=True)
     scale = jnp.sqrt((grad_square + GRAFT_EPS) / (update_square + GRAFT_EPS))
-    usend[...] = (uflip[...] * scale).astype(BF16).reshape(usend.shape)
-
-    def update_copy(off):
-        to = (b + off) % owners
-        return remote(usend.at[to], uland.at[group, member], up_send, up_recv, blk=to)
-
-    @pl.loop(1, owners)
-    def _(off):
-        update_copy(off).start()
-
-    pltpu.make_async_copy(usend.at[b], uland.at[group, member], up_recv).start()
+    scales[group] = jnp.broadcast_to(scale, (8, 128))
+
+    def scale_copy(off):
+        to = (group + off) % groups
+        return remote(
+            scales.at[group],
+            scales.at[group],
+            sc_send.at[off],
+            sc_recv.at[off],
+            blk=to * GROUP + member,
+        )
+
+    for off in range(1, groups):
+        scale_copy(off).start()
 
     loads[3].wait()
     first = pl.ds(pl.multiple_of(member * slab, slab), slab)
-    columns = gbuf[:, :, :, :, first].reshape(width, slab).T
+    columns = gbuf[:, :, :, :, :, first].reshape(width, slab).T
 
     @pl.loop(0, tiles)
     def _(step):
         cols = pl.ds(pl.multiple_of(step * tile, tile), tile)
-        grad = gbuf[:, :, :, :, cols].reshape(width, tile)
+        grad = gbuf[:, :, :, :, :, cols].reshape(width, tile)
         gram = jnp.dot(columns, grad, preferred_element_type=F32)
         rstat[:, cols] = STAT_DECAY * rstat[:, cols] + (1.0 - STAT_DECAY) * gram
 
@@ -464,20 +507,26 @@
         x_copy(0, route).wait_send()
         x_copy(1, route).wait_send()
     qgather.drain()
-    for spread in spreads[:-1]:
+    for spread in spreads:
         spread.wait_send()
     pl.when(chip < 3)(lambda: pass_copy(chip, 0).wait_send())
     pl.when(chip > 0)(lambda: pass_copy(chip, 1).wait_send())
     passing(sent)
-    lane = gbuf.at[:, :, core]
-    pltpu.make_async_copy(lane, lane, sib_send).wait()
+    for slot in range(16):
+        pass_copy(slot, 2).wait_send()
     for off in range(1, GROUP):
         square_copy(off).wait_send()
+    for off in range(1, groups):
+        scale_copy(off).wait_send()
+        scale_copy(off).wait_recv()
 
     pltpu.make_async_copy(uland, uland, up_recv).wait()
     for block in range(groups):
+        factor = scales[block, 0:1]
         for part in range(GROUP):
-            ubuf[block, :, part * slab : (part + 1) * slab] = uland[block, part]
+            ubuf[block, :, part * slab : (part + 1) * slab] = (
+                uland[block, part].astype(F32) * factor
+            ).astype(BF16)
     store_update = pltpu.make_async_copy(ubuf, update_ref, out_sem.at[2])
     store_update.start()
     others = usend.at[pl.ds(0, owners - 1)]
@@ -501,7 +550,7 @@
             jax.ShapeDtypeStruct((slab, width), F32),
             jax.ShapeDtypeStruct((slab, width), F32),
         ),
-        in_specs=[pl.BlockSpec(memory_space=pl.ANY)] * 5,
+        in_specs=[pl.BlockSpec(memory_space=pltpu.HBM)] * 5,
         out_specs=[pl.BlockSpec(memory_space=pl.ANY)] * 3,
         scratch_shapes=[
             pltpu.VMEM((row_count, replicas, local, width), BF16),
@@ -509,16 +558,17 @@
             *[pltpu.VMEM((2, row_count // 2, local, width), BF16)] * 3,
             pltpu.VMEM((width // 128, row_count * local, 128), F32),
             pltpu.VMEM((local, row_count, width), BF16),
-            pltpu.VMEM((2, 16, 2, row_count, width), BF16),
+            pltpu.VMEM((4, 2, 4, 2, row_count, width), BF16),
             pltpu.VMEM((GROUP, slab, width), BF16),
             pltpu.VMEM((slab, width), BF16),
             pltpu.VMEM((slab, width), F32),
             pltpu.VMEM((slab, width), F32),
+            pltpu.VMEM((slab, width), F32),
             pltpu.VMEM((slab, width), BF16),
-            pltpu.VMEM((width, slab), F32),
             pltpu.VMEM((owners, part, slab), BF16),
             pltpu.VMEM((groups, GROUP, part, slab), BF16),
             pltpu.VMEM((GROUP, 16, 128), F32),
+            pltpu.VMEM((groups, 8, 128), F32),
             pltpu.VMEM((local, part, width), BF16),
             dma((4,)),
             dma((GROUP,)),
@@ -531,26 +581,33 @@
             dma((2, 4)),
             dma((2, 16)),
             dma((16,)),
-            dma,
-            dma,
+            dma((16,)),
+            dma((16,)),
             dma((GROUP,)),
             dma((GROUP,)),
+            dma((groups,)),
+            dma((groups,)),
             dma,
             dma,
             dma((3,)),
         ],
         compiler_params=pltpu.CompilerParams(
-            collective_id=0, has_side_effects=True, vmem_limit_bytes=60 * 2**20
+            collective_id=0, has_side_effects=True, vmem_limit_bytes=40 * 2**20
         ),
         cost_estimate=pl.CostEstimate(
             flops=8 * slab * width * width, bytes_accessed=8 * 2**20, transcendentals=0
         ),
     )(
-        gradients.reshape(row_count, replicas, local, width),
-        left_stat[0],
-        right_stat[0],
-        left_root[0],
-        right_root[0],
+        *(
+            pltpu.with_memory_space_constraint(x, pltpu.HBM)
+            for x in (
+                gradients.reshape(row_count, replicas, local, width),
+                left_stat[0],
+                right_stat[0],
+                left_root[0],
+                right_root[0],
+            )
+        )
     )
     return jnp.swapaxes(update, 1, 2), new_left[None], new_right[None]
 

time: 109 us -> 104 us (0.954)
  local copies, waits for them, and re-layouts: 5.44 us -> 2.29 us
  Pallas kernels: 103 us -> 101 us
    unnamed x3, local copies, waits for them, and re-layouts: 5.44 us -> 2.29 us
    pallas_call x1, Pallas kernels: 103 us -> 101 us  [on_device(): pl.pallas_call(functools.partial(kernel, replicas, owners), out_shape=(ja...]
where the time goes in v4:
time: 104 us; the launch traced here: 103 us
  Pallas kernels  101 us (97%)
  local copies, waits for them, and re-layouts  2.29 us (2%)
    pallas_call x1, Pallas kernels, on_device(): pl.pallas_call(functools.partial(kernel, replicas, owners), out_shape=(ja...  101 us
    unnamed x3, local copies, waits for them, and re-layouts  2.29 us

profile of v4, /device:TPU:1, one launch (start us, length us, event | category | flops | bytes accessed | tf_op | source)
XLA Modules:
  0.0 103.4 jit_solution(16465336224107856905)
XLA Ops:
  0.6 100.5 %shard_map.76 = (bf16[8,16,1024]{2,1,0:T(8,128)(2,1)S(1)}, f32[128,1024]{1,0:T(8,128)S(1)}, f32[128,1024]{1,0:T(8,128)S(1)}) custom-call(bf16[16,8,8,1024]{3,2,1,0:T(8,128)(2,1)} %bitcast.11, f32[128,1024]{1,0:T(8,128)} %bitcast.12, f32[128,1024]{1,0:T(8,128)} %bitcast.13, bf16[128,1024]{1,0:T(8,128)(2,1)} %bitcast.14, bf16[128,1024]{1,0:T(8,128)(2,1)} %bitcast.15), custom_call_target="tpu_custom_call" | custom-call | flops 1073741824 | bytes 8388608 | tf_op jit(solution)/shard_map/pallas_call | solution.py:546
  101.1 0.7 copy.11
  101.9 0.8 copy.12
  102.6 0.8 copy.13

commit v5 on v4

--- a/solution.py
+++ b/solution.py
@@ -27,71 +27,45 @@
 
 
 class LineGather:
-    def __init__(self, view, group, member, send, recv):
-        self.view, self.group, self.member = view, group, member
+    def __init__(self, view, first, chip, send, recv):
+        self.view, self.first, self.chip = view, first, chip
         self.send, self.recv = send, recv
-        self.chip, self.core = member // 2, member % 2
-
-    def copy(self, slot, target, way):
+
+    def copy(self, slot, way):
+        target = self.chip + (1 if way == 0 else -1)
         return remote(
             self.view(slot),
             self.view(slot),
             self.send.at[slot, way],
             self.recv.at[slot],
-            blk=self.group * GROUP + target,
-        )
-
-    def to_right(self, slot):
-        return self.copy(slot, self.member + 2, 0)
-
-    def to_left(self, slot):
-        return self.copy(slot, self.member - 2, 1)
-
-    def to_sibling(self, slot):
-        return self.copy(slot, self.chip * 2 + 1 - self.core, 2)
+            blk=self.first + 2 * target,
+        )
 
     def own(self):
-        slot = self.member
-        pl.when(self.chip < 3)(lambda: self.to_right(slot).start())
-        pl.when(self.chip > 0)(lambda: self.to_left(slot).start())
-        self.to_sibling(slot).start()
+        pl.when(self.chip < 3)(lambda: self.copy(self.chip, 0).start())
+        pl.when(self.chip > 0)(lambda: self.copy(self.chip, 1).start())
 
     def hop(self, hop):
-        left, right = self.member - 2 * hop, self.member + 2 * hop
-
-        @pl.when(self.chip >= hop)
+        left, right = self.chip - hop, self.chip + hop
+
+        @pl.when(left >= 0)
         def _():
-            self.to_right(left).wait_recv()
-            pl.when(self.chip < 3)(lambda: self.to_right(left).start())
-            self.to_sibling(left).start()
-
-        @pl.when(self.chip + hop <= 3)
+            self.copy(left, 0).wait_recv()
+            pl.when(self.chip < 3)(lambda: self.copy(left, 0).start())
+
+        @pl.when(right <= 3)
         def _():
-            self.to_left(right).wait_recv()
-            pl.when(self.chip > 0)(lambda: self.to_left(right).start())
-            self.to_sibling(right).start()
-
-    def finish(self):
-        for other in range(4):
-            self.to_sibling(other * 2 + 1 - self.core).wait_recv()
+            self.copy(right, 1).wait_recv()
+            pl.when(self.chip > 0)(lambda: self.copy(right, 1).start())
 
     def drain(self):
         chip = self.chip
-        pl.when(chip < 3)(lambda: self.to_right(self.member).wait_send())
-        pl.when(chip > 0)(lambda: self.to_left(self.member).wait_send())
-        self.to_sibling(self.member).wait_send()
+        pl.when(chip < 3)(lambda: self.copy(chip, 0).wait_send())
+        pl.when(chip > 0)(lambda: self.copy(chip, 1).wait_send())
         for hop in range(1, 4):
-            left, right = self.member - 2 * hop, self.member + 2 * hop
-
-            @pl.when(chip >= hop)
-            def _():
-                pl.when(chip < 3)(lambda: self.to_right(left).wait_send())
-                self.to_sibling(left).wait_send()
-
-            @pl.when(chip + hop <= 3)
-            def _():
-                pl.when(chip > 0)(lambda: self.to_left(right).wait_send())
-                self.to_sibling(right).wait_send()
+            left, right = chip - hop, chip + hop
+            pl.when((left >= 0) & (chip < 3))(lambda: self.copy(left, 0).wait_send())
+            pl.when((right <= 3) & (chip > 0))(lambda: self.copy(right, 1).wait_send())
 
 
 def kernel(
@@ -133,6 +107,8 @@
     y_recv,
     x_send,
     x_recv,
+    pair_send,
+    pair_recv,
     qg_send,
     qg_recv,
     sp_send,
@@ -161,9 +137,20 @@
     tile = 256
     tiles = width // tile
 
+    pair = group * GROUP + chip * 2
+    sibling = pair + 1 - core
+
+    def half_of(which):
+        return pl.ds(pl.multiple_of(which * (width // 2), width // 2), width // 2)
+
+    def part_of(which):
+        return pl.ds(pl.multiple_of(which * slab, slab), slab)
+
     loads = [
         pltpu.make_async_copy(grad_ref, gown, local_sem.at[0]),
-        pltpu.make_async_copy(rroot_ref, qbuf.at[member], local_sem.at[1]),
+        pltpu.make_async_copy(
+            rroot_ref.at[:, half_of(core)], qbuf.at[chip, part_of(core)], local_sem.at[1]
+        ),
         pltpu.make_async_copy(left_ref, lstat, local_sem.at[2]),
         pltpu.make_async_copy(right_ref, rstat, local_sem.at[3]),
     ]
@@ -172,12 +159,12 @@
         loads.append(
             pltpu.make_async_copy(
                 lroot_ref.at[:, pl.ds(pl.multiple_of(natural * 128, 128), 128)],
-                proot.at[:, pl.ds(block * 128, 128)],
+                proot.at[part_of(core), pl.ds(block * 128, 128)],
                 root_sem.at[block],
             )
         )
-    loads[0].start()
-    loads[1].start()
+    for load in loads:
+        load.start()
 
     flip = (b + owners // 2) % owners
     turn = y * 2 + 1 - xh
@@ -230,34 +217,52 @@
         return remote(src, dst, x_send.at[stage, route], x_recv.at[stage, route], **where)
 
     ways = (0, 1)
+    for which in (0, 1):
+        for way in ways:
+            y_copy(0, way, which).start()
+
+    root_swap = remote(
+        rroot_ref.at[:, half_of(1 - core)],
+        qbuf.at[chip, part_of(core)],
+        pair_send.at[0],
+        pair_recv.at[0],
+        blk=sibling,
+    )
+    root_swap.start()
+    for load in loads[4:]:
+        load.wait()
+    factor_swap = remote(
+        proot.at[part_of(core)],
+        proot.at[part_of(core)],
+        pair_send.at[1],
+        pair_recv.at[1],
+        blk=sibling,
+    )
+    factor_swap.start()
+    loads[1].wait()
+    root_swap.wait_recv()
+    qgather = LineGather(
+        lambda s: qbuf.at[s], group * GROUP + core, chip, qg_send, qg_recv
+    )
+    qgather.own()
+    loads[0].wait()
+
+    def y_add(way, which):
+        y_copy(0, way, which).wait_recv()
+
+        @pl.loop(0, half)
+        def _(row):
+            mine = gown[way * half + row, at_y(steps[way], sides[which])]
+            passed = yfar[way, which, row]
+            yadd[way, which, row] = (mine.astype(F32) + passed.astype(F32)).astype(BF16)
+
     for way in ways:
-        y_copy(0, way, 0).start()
+        y_add(way, 0)
+        y_copy(2, way, 0).start()
     for way in ways:
         y_copy(1, way, 0).start()
-        y_copy(0, way, 1).start()
-
-    loads[1].wait()
-    qgather = LineGather(lambda s: qbuf.at[s], group, member, qg_send, qg_recv)
-    qgather.own()
-    for load in loads[2:]:
-        load.start()
-    loads[0].wait()
-
-    for which in (0, 1):
-        for way in ways:
-            y_copy(0, way, which).wait_recv()
-
-            @pl.loop(0, half)
-            def _(row):
-                mine = gown[way * half + row, at_y(steps[way], sides[which])]
-                passed = yfar[way, which, row]
-                yadd[way, which, row] = (mine.astype(F32) + passed.astype(F32)).astype(BF16)
-
-            y_copy(2, way, which).start()
-        if which == 0:
-            for way in ways:
-                y_copy(1, way, 1).start()
-    qgather.hop(1)
+    for way in ways:
+        y_add(way, 1)
 
     def y_total(part, which, row):
         return (
@@ -275,6 +280,10 @@
             xout[part, row] = y_total(part, 0, row).astype(BF16)
 
         x_copy(0, part).start()
+    for kind in (2, 1):
+        for way in ways:
+            y_copy(kind, way, 1).start()
+    qgather.hop(1)
     for route in ways:
         x_copy(0, route).wait_recv()
         x_copy(1, route).start()
@@ -321,32 +330,45 @@
     def slot_view(slot, which=core):
         return gbuf.at[slot // 4, :, slot % 4, which]
 
-    spreads = [spread_copy(1, 0)]
-    spreads += [spread_copy(across, ahead) for ahead in (2, 1, 3) for across in (1, 0)]
-    for spread in spreads:
-        spread.start()
+    reach = {1: 4 - chip, 3: chip + 1, 2: jnp.where((chip == 1) | (chip == 2), 6, 5)}
+
+    def spread_to(distance, action):
+        for ahead, lowest, highest in ((1, 1, 4), (3, 1, 4), (2, 5, 6)):
+            if lowest <= distance <= highest:
+
+                @pl.when(reach[ahead] == distance)
+                def _():
+                    for across in (0, 1):
+                        action(spread_copy(across, ahead))
+
+    spread_copy(1, 0).start()
+    spread_to(1, lambda copy: copy.start())
+    spread_to(2, lambda copy: copy.start())
     own_slot = gbuf.at[0, xl, chip, core]
     pltpu.make_async_copy(summed.at[group], own_slot, gg_recv.at[chip]).start()
 
     def pass_copy(slot, way):
         view = slot_view(slot)
-        if way == 2:
-            return remote(view, view, sib_send.at[slot], sib_recv.at[slot], blk=group * GROUP + chip * 2 + 1 - core)
         target = member + 2 if way == 0 else member - 2
         return remote(
             view, view, gg_send.at[way, slot], gg_recv.at[slot], blk=group * GROUP + target
         )
 
+    def cross_slot(slot):
+        view = slot_view(slot)
+        return remote(view, view, sib_send.at[slot], sib_recv.at[slot], blk=sibling)
+
+    def cross_quad(quad):
+        view = gbuf.at[quad, :, :, core]
+        return remote(view, view, sib_send.at[quad], sib_recv.at[quad], blk=sibling)
+
     def wait_slot(slot):
         view = slot_view(slot)
         pltpu.make_async_copy(view, view, gg_recv.at[slot]).wait()
 
-    qgather.hop(3)
-
     wait_slot(chip)
     pl.when(chip < 3)(lambda: pass_copy(chip, 0).start())
     pl.when(chip > 0)(lambda: pass_copy(chip, 1).start())
-    pass_copy(chip, 2).start()
 
     def passing(action, between=None):
         for step in range(1, 10):
@@ -360,15 +382,19 @@
     def forward(slot, way, more):
         wait_slot(slot)
         pl.when(more)(lambda: pass_copy(slot, way).start())
-        pass_copy(slot, 2).start()
+        pl.when(slot // 4 == 2)(lambda: cross_slot(slot).start())
 
     def sent(slot, way, more):
         pl.when(more)(lambda: pass_copy(slot, way).wait_send())
 
     def apply_quad(quad, first):
-        for slot in range(quad * 4, quad * 4 + 4):
-            view = slot_view(slot, 1 - core)
-            pltpu.make_async_copy(view, view, sib_recv.at[slot]).wait()
+        if quad == 2:
+            for slot in range(8, 12):
+                view = slot_view(slot, 1 - core)
+                pltpu.make_async_copy(view, view, sib_recv.at[slot]).wait()
+        else:
+            view = gbuf.at[quad, :, :, 1 - core]
+            pltpu.make_async_copy(view, view, sib_recv.at[quad]).wait()
         factor = proot[:, quad * 256 : (quad + 1) * 256]
 
         @pl.loop(0, tiles)
@@ -384,42 +410,51 @@
                 lacc[:, cols] = part
 
     def compute(step):
-        if step == 4:
-            for load in loads[4:]:
-                load.wait()
+        if step <= 4:
+            spread_to(step + 2, lambda copy: copy.start())
+        if step == 3:
+            cross_quad(0).start()
+        elif step == 5:
+            factor_swap.wait_recv()
             apply_quad(0, True)
         elif step == 7:
+            cross_quad(1).start()
+            cross_quad(3).start()
+        elif step == 9:
             apply_quad(1, False)
-        elif step == 8:
             apply_quad(3, False)
 
     passing(forward, compute)
-    qgather.finish()
     apply_quad(2, False)
+    qgather.hop(3)
 
     applied = lapp[...]
     squares[member] = jnp.zeros((16, 128), F32)
-    per_tile = owners // tiles
-
-    def update_copy(to):
-        return remote(usend.at[to], uland.at[group, member], up_send, up_recv, blk=to)
-
-    mine = pltpu.make_async_copy(usend.at[b], uland.at[group, member], up_recv)
-    for turn_tile in (1, 2, 3, 0):
-        number = (b // per_tile + turn_tile) % tiles
+    ends = owners // 2
+    per_tile = ends // 2
+
+    def update_copy(end):
+        return remote(
+            usend.at[end], uland.at[group, chip], up_send, up_recv, blk=core * ends + end
+        )
+
+    mine = pltpu.make_async_copy(usend.at[b % ends], uland.at[group, chip], up_recv)
+    for turn_tile in (1, 0):
+        number = (b % ends // per_tile + turn_tile) % 2
         cols = pl.ds(pl.multiple_of(number * tile, tile), tile)
         part = jnp.dot(
             applied, qbuf[:, :, cols].reshape(width, tile), preferred_element_type=F32
         )
         flipped = part.T
         usend[pl.ds(number * per_tile, per_tile)] = flipped.astype(BF16).reshape(
-            per_tile, tile // per_tile, slab
+            per_tile, tile // per_tile, 2 * slab
         )
         squares[member, 8:16] += jnp.sum(
-            (flipped * flipped).reshape(tile // 8, 8, slab), axis=0
+            (flipped * flipped).reshape(tile // 8, 8, 2, slab), axis=(0, 2)
         )
         if turn_tile == 0:
-            mine.start()
+            pl.when(xl == core)(lambda: mine.start())
+            pl.when(xl != core)(lambda: update_copy(b % ends).start())
 
         @pl.loop(1 if turn_tile == 0 else 0, per_tile)
         def _(off):
@@ -507,13 +542,18 @@
         x_copy(0, route).wait_send()
         x_copy(1, route).wait_send()
     qgather.drain()
-    for spread in spreads:
-        spread.wait_send()
+    root_swap.wait_send()
+    factor_swap.wait_send()
+    spread_copy(1, 0).wait_send()
+    for distance in range(1, 7):
+        spread_to(distance, lambda copy: copy.wait_send())
     pl.when(chip < 3)(lambda: pass_copy(chip, 0).wait_send())
     pl.when(chip > 0)(lambda: pass_copy(chip, 1).wait_send())
     passing(sent)
-    for slot in range(16):
-        pass_copy(slot, 2).wait_send()
+    for quad in (0, 1, 3):
+        cross_quad(quad).wait_send()
+    for slot in range(8, 12):
+        cross_slot(slot).wait_send()
     for off in range(1, GROUP):
         square_copy(off).wait_send()
     for off in range(1, groups):
@@ -524,13 +564,15 @@
     for block in range(groups):
         factor = scales[block, 0:1]
         for part in range(GROUP):
+            piece = uland[block, part // 2, :, part % 2 * slab : (part % 2 + 1) * slab]
             ubuf[block, :, part * slab : (part + 1) * slab] = (
-                uland[block, part].astype(F32) * factor
+                piece.astype(F32) * factor
             ).astype(BF16)
     store_update = pltpu.make_async_copy(ubuf, update_ref, out_sem.at[2])
     store_update.start()
-    others = usend.at[pl.ds(0, owners - 1)]
-    pltpu.make_async_copy(others, others, up_send).wait()
+    others = usend.at[pl.ds(0, ends - 1)]
+    pl.when(xl == core)(lambda: pltpu.make_async_copy(others, others, up_send).wait())
+    pl.when(xl != core)(lambda: pltpu.make_async_copy(usend, usend, up_send).wait())
     store_left.wait()
     store_right.wait()
     store_update.wait()
@@ -559,14 +601,14 @@
             pltpu.VMEM((width // 128, row_count * local, 128), F32),
             pltpu.VMEM((local, row_count, width), BF16),
             pltpu.VMEM((4, 2, 4, 2, row_count, width), BF16),
-            pltpu.VMEM((GROUP, slab, width), BF16),
-            pltpu.VMEM((slab, width), BF16),
+            pltpu.VMEM((4, 2 * slab, width // 2), BF16),
+            pltpu.VMEM((2 * slab, width), BF16),
             pltpu.VMEM((slab, width), F32),
             pltpu.VMEM((slab, width), F32),
-            pltpu.VMEM((slab, width), F32),
-            pltpu.VMEM((slab, width), BF16),
-            pltpu.VMEM((owners, part, slab), BF16),
-            pltpu.VMEM((groups, GROUP, part, slab), BF16),
+            pltpu.VMEM((2 * slab, width), F32),
+            pltpu.VMEM((2 * slab, width), BF16),
+            pltpu.VMEM((owners // 2, part, 2 * slab), BF16),
+            pltpu.VMEM((groups, 4, part, 2 * slab), BF16),
             pltpu.VMEM((GROUP, 16, 128), F32),
             pltpu.VMEM((groups, 8, 128), F32),
             pltpu.VMEM((local, part, width), BF16),
@@ -576,8 +618,10 @@
             dma((3, 2, 2)),
             dma((2, 2)),
             dma((2, 2)),
-            dma((GROUP, 3)),
-            dma((GROUP,)),
+            dma((2,)),
+            dma((2,)),
+            dma((4, 2)),
+            dma((4,)),
             dma((2, 4)),
             dma((2, 16)),
             dma((16,)),

time: 104 us -> 106 us (1.019)
  Pallas kernels: 101 us -> 103 us
    pallas_call x1, Pallas kernels: 101 us -> 103 us  [on_device(): pl.pallas_call(functools.partial(kernel, replicas, owners), out_shape=(ja...]
where the time goes in v5:
time: 106 us
  Pallas kernels  103 us (97%)
  local copies, waits for them, and re-layouts  2.29 us (2%)
    pallas_call x1, Pallas kernels, on_device(): pl.pallas_call(functools.partial(kernel, replicas, owners), out_shape=(ja...  103 us
    unnamed x3, local copies, waits for them, and re-layouts  2.29 us

profile of v5, /device:TPU:1, one launch (start us, length us, event | category | flops | bytes accessed | tf_op | source)
XLA Modules:
  0.0 106.1 jit_solution(6304176268198205190)
XLA Ops:
  0.6 103.2 %shard_map.76 = (bf16[8,16,1024]{2,1,0:T(8,128)(2,1)S(1)}, f32[128,1024]{1,0:T(8,128)S(1)}, f32[128,1024]{1,0:T(8,128)S(1)}) custom-call(bf16[16,8,8,1024]{3,2,1,0:T(8,128)(2,1)} %bitcast.11, f32[128,1024]{1,0:T(8,128)} %bitcast.12, f32[128,1024]{1,0:T(8,128)} %bitcast.13, bf16[128,1024]{1,0:T(8,128)(2,1)} %bitcast.14, bf16[128,1024]{1,0:T(8,128)(2,1)} %bitcast.15), custom_call_target="tpu_custom_call" | custom-call | flops 1073741824 | bytes 8388608 | tf_op jit(solution)/shard_map/pallas_call | solution.py:588
  103.8 0.7 copy.11
  104.5 0.8 copy.12
  105.3 0.8 copy.13

commit v6 on v5

v6 whole, which is shorter than its diff:
```python
import functools

import jax
import jax.numpy as jnp
from jax import lax
from jax.experimental import pallas as pl
from jax.experimental.pallas import tpu as pltpu
from jax.sharding import PartitionSpec as P

GROUP = 8
STAT_DECAY = 0.95
GRAFT_EPS = 1e-06
MESH = pl.DeviceIdType.MESH
F32 = jnp.float32
BF16 = jnp.bfloat16


def remote(src, dst, send, recv, **where):
    return pltpu.make_async_remote_copy(
        src_ref=src,
        dst_ref=dst,
        send_sem=send,
        recv_sem=recv,
        device_id=where,
        device_id_type=MESH,
    )


class LineGather:
    def __init__(self, view, first, chip, send, recv):
        self.view, self.first, self.chip = view, first, chip
        self.send, self.recv = send, recv

    def copy(self, slot, way):
        target = self.chip + (1 if way == 0 else -1)
        return remote(
            self.view(slot),
            self.view(slot),
            self.send.at[slot, way],
            self.recv.at[slot],
            blk=self.first + 2 * target,
        )

    def own(self):
        pl.when(self.chip < 3)(lambda: self.copy(self.chip, 0).start())
        pl.when(self.chip > 0)(lambda: self.copy(self.chip, 1).start())

    def hop(self, hop):
        left, right = self.chip - hop, self.chip + hop

        @pl.when(left >= 0)
        def _():
            self.copy(left, 0).wait_recv()
            pl.when(self.chip < 3)(lambda: self.copy(left, 0).start())

        @pl.when(right <= 3)
        def _():
            self.copy(right, 1).wait_recv()
            pl.when(self.chip > 0)(lambda: self.copy(right, 1).start())

    def drain(self):
        chip = self.chip
        pl.when(chip < 3)(lambda: self.copy(chip, 0).wait_send())
        pl.when(chip > 0)(lambda: self.copy(chip, 1).wait_send())
        for hop in range(1, 4):
            left, right = chip - hop, chip + hop
            pl.when((left >= 0) & (chip < 3))(lambda: self.copy(left, 0).wait_send())
            pl.when((right <= 3) & (chip > 0))(lambda: self.copy(right, 1).wait_send())


def kernel(
    replicas,
    owners,
    grad_ref,
    left_ref,
    right_ref,
    lroot_ref,
    rroot_ref,
    update_ref,
    newl_ref,
    newr_ref,
    land,
    fsum,
    summed,
    gbuf,
    qbuf,
    proot,
    lstat,
    rstat,
    lapp,
    usend,
    uland,
    squares,
    scales,
    ubuf,
    local_sem,
    own_sem,
    root_sem,
    rs_send,
    rs_recv,
    pair_send,
    pair_recv,
    qg_send,
    qg_recv,
    sp_send,
    gg_send,
    gg_recv,
    sib_send,
    sib_recv,
    sq_send,
    sq_recv,
    sc_send,
    sc_recv,
    up_send,
    up_recv,
    out_sem,
):
    p = lax.axis_index("dp")
    b = lax.axis_index("blk")
    groups = owners // GROUP
    group, member = b // GROUP, b % GROUP
    chip, core = member // 2, member % 2
    xl, quarter = group // 4, group % 4
    row_count, width = grad_ref.shape[0], grad_ref.shape[3]
    half = width // 2
    slab = width // GROUP
    tile = 256
    tiles = width // tile

    pair = group * GROUP + chip * 2
    sibling = pair + 1 - core

    def half_of(which):
        return pl.ds(pl.multiple_of(which * (width // 2), width // 2), width // 2)

    def part_of(which):
        return pl.ds(pl.multiple_of(which * slab, slab), slab)

    loads = [
        pltpu.make_async_copy(
            rroot_ref.at[:, half_of(core)], qbuf.at[chip, part_of(core)], local_sem.at[0]
        ),
        pltpu.make_async_copy(left_ref, lstat, local_sem.at[1]),
        pltpu.make_async_copy(right_ref, rstat, local_sem.at[2]),
    ]
    own_land = [
        pltpu.make_async_copy(
            grad_ref.at[:, p, :, pl.ds(part * half, half)], land.at[part, 0], own_sem.at[part]
        )
        for part in (0, 1)
    ]
    for block in range(GROUP):
        natural = (block % 2) * 4 + (block // 2 + quarter) % 4
        loads.append(
            pltpu.make_async_copy(
                lroot_ref.at[:, pl.ds(pl.multiple_of(natural * 128, 128), 128)],
                proot.at[part_of(core), pl.ds(block * 128, 128)],
                root_sem.at[block],
            )
        )
    for load in loads + own_land:
        load.start()

    barrier = pltpu.get_barrier_semaphore()
    for off in range(1, replicas):
        pl.semaphore_signal(
            barrier, inc=1, device_id={"dp": (p + off) % replicas}, device_id_type=MESH
        )

    @pl.loop(1, owners)
    def _(off):
        pl.semaphore_signal(
            barrier, inc=1, device_id={"blk": (b + off) % owners}, device_id_type=MESH
        )

    pl.semaphore_wait(barrier, replicas - 1 + owners - 1)

    def reduce_copy(part, off):
        to = (p + off) % replicas
        return remote(
            grad_ref.at[:, to, :, pl.ds(part * half, half)],
            land.at[part, off],
            rs_send.at[part, off],
            rs_recv.at[part, off],
            dp=to,
        )

    for off in range(1, replicas):
        reduce_copy(0, off).start()

    root_swap = remote(
        rroot_ref.at[:, half_of(1 - core)],
        qbuf.at[chip, part_of(core)],
        pair_send.at[0],
        pair_recv.at[0],
        blk=sibling,
    )
    root_swap.start()
    for load in loads[3:]:
        load.wait()
    factor_swap = remote(
        proot.at[part_of(core)],
        proot.at[part_of(core)],
        pair_send.at[1],
        pair_recv.at[1],
        blk=sibling,
    )
    factor_swap.start()
    loads[0].wait()
    root_swap.wait_recv()
    qgather = LineGather(
        lambda s: qbuf.at[s], group * GROUP + core, chip, qg_send, qg_recv
    )
    qgather.own()

    def sum_part(part):
        own_land[part].wait()

        @pl.loop(0, row_count)
        def _(row):
            total = land[part, 0, row].astype(F32)
            for off in range(1, replicas):
                total = total + land[part, off, row].astype(F32)
            place = pl.ds(pl.multiple_of(row * groups, groups), groups)
            for lane in range(half // 128):
                fsum[lane, place, :] = total[:, lane * 128 : (lane + 1) * 128]

        for block in range(groups):
            for lane in range(half // 128):
                summed[part, block, :, lane * 128 : (lane + 1) * 128] = fsum[
                    lane, pl.ds(block, row_count, stride=groups), :
                ].astype(BF16)

    for off in range(1, 5):
        reduce_copy(0, off).wait_recv()
    for off in range(1, replicas):
        reduce_copy(1, off).start()
    for off in range(5, replicas):
        reduce_copy(0, off).wait_recv()
    sum_part(0)

    def spread_copy(part, across, ahead):
        to_quarter = (quarter + ahead) % 4
        to_xl = (xl + across) % 2
        slot = (chip - 4 * ahead) % 16
        if ahead == 0:
            entry = chip
        elif ahead == 1:
            entry = 0
        elif ahead == 3:
            entry = 3
        else:
            entry = jnp.where(chip <= 1, 3, 0)
        return remote(
            summed.at[part, to_xl * 4 + to_quarter],
            gbuf.at[part, slot // 4, xl, slot % 4, core],
            sp_send.at[part, across, ahead],
            gg_recv.at[part, slot],
            blk=((to_xl * 4 + to_quarter) * 4 + entry) * 2 + core,
        )

    def slot_view(part, slot):
        return gbuf.at[part, slot // 4, :, slot % 4, core]

    spread_order = [(1, 0)] + [(across, ahead) for ahead in (1, 3, 2) for across in (1, 0)]

    def spread_part(part):
        for across, ahead in spread_order:
            spread_copy(part, across, ahead).start()
        pltpu.make_async_copy(
            summed.at[part, group], gbuf.at[part, 0, xl, chip, core], gg_recv.at[part, chip]
        ).start()

    def pass_copy(part, slot, way):
        view = slot_view(part, slot)
        target = member + 2 if way == 0 else member - 2
        return remote(
            view,
            view,
            gg_send.at[part, way, slot],
            gg_recv.at[part, slot],
            blk=group * GROUP + target,
        )

    def cross_quad(part, quad):
        view = gbuf.at[part, quad, :, :, core]
        return remote(
            view, view, sib_send.at[part, quad], sib_recv.at[part, quad], blk=sibling
        )

    def wait_slot(part, slot):
        view = slot_view(part, slot)
        pltpu.make_async_copy(view, view, gg_recv.at[part, slot]).wait()

    def at_step(step, action):
        if step == 0:
            action(chip, 0, chip < 3, False)
            action(chip, 1, chip > 0, False)
            return
        from_left = (chip - step + 16) % 16
        from_right = chip + step
        pl.when(step <= chip + 6)(lambda: action(from_left, 0, chip < 3, True))
        pl.when(step <= 9 - chip)(lambda: action(from_right, 1, chip > 0, True))

    def hand_on(part, step):
        def forward(slot, way, more, arrives):
            if arrives:
                wait_slot(part, slot)
            pl.when(more)(lambda: pass_copy(part, slot, way).start())

        if step == 0:
            wait_slot(part, chip)
        at_step(step, forward)
        if step == 3:
            cross_quad(part, 0).start()
        elif step == 7:
            cross_quad(part, 1).start()
            cross_quad(part, 3).start()
        elif step == 9:
            cross_quad(part, 2).start()

    def handed_on(part, step):
        def sent(slot, way, more, arrives):
            pl.when(more)(lambda: pass_copy(part, slot, way).wait_send())

        at_step(step, sent)

    def apply_part(part):
        for quad in range(4):
            view = gbuf.at[part, quad, :, :, 1 - core]
            pltpu.make_async_copy(view, view, sib_recv.at[part, quad]).wait()

        @pl.loop(0, half // tile)
        def _(step):
            cols = pl.ds(pl.multiple_of(step * tile, tile), tile)
            grad = gbuf[part, :, :, :, :, :, cols].reshape(width, tile)
            to = pl.ds(pl.multiple_of(part * half + step * tile, tile), tile)
            lapp[:, to] = jnp.dot(proot[...], grad, preferred_element_type=F32).astype(BF16)

    spread_part(0)
    qgather.hop(1)
    for step in range(3):
        hand_on(0, step)
    qgather.hop(2)
    for off in range(1, replicas):
        reduce_copy(1, off).wait_recv()
    sum_part(1)
    spread_part(1)
    factor_swap.wait_recv()
    for step in range(3, 10):
        hand_on(0, step)
        hand_on(1, step - 3)
    hand_on(1, 7)
    apply_part(0)
    hand_on(1, 8)
    hand_on(1, 9)
    qgather.hop(3)
    apply_part(1)

    applied = lapp[...]
    squares[member] = jnp.zeros((16, 128), F32)
    ends = owners // 2
    per_tile = ends // 2

    def update_copy(end):
        return remote(
            usend.at[end], uland.at[group, chip], up_send, up_recv, blk=core * ends + end
        )

    mine = pltpu.make_async_copy(usend.at[b % ends], uland.at[group, chip], up_recv)
    for turn_tile in (1, 0):
        number = (b % ends // per_tile + turn_tile) % 2
        cols = pl.ds(pl.multiple_of(number * tile, tile), tile)
        part = jnp.dot(
            applied, qbuf[:, :, cols].reshape(width, tile), preferred_element_type=F32
        )
        flipped = part.T
        usend[pl.ds(number * per_tile, per_tile)] = flipped.astype(BF16).reshape(
            per_tile, tile // per_tile, 2 * slab
        )
        squares[member, 8:16] += jnp.sum(
            (flipped * flipped).reshape(tile // 8, 8, 2, slab), axis=(0, 2)
        )
        if turn_tile == 0:
            pl.when(xl == core)(lambda: mine.start())
            pl.when(xl != core)(lambda: update_copy(b % ends).start())

        @pl.loop(1 if turn_tile == 0 else 0, per_tile)
        def _(off):
            update_copy(number * per_tile + (b + off) % per_tile).start()

    my_quad = (member % 4 - quarter + 4) % 4
    squares[member, 0:8] = jnp.zeros((8, 128), F32)
    for part in (0, 1):
        wide = gbuf[part, my_quad, member // 4].reshape(slab, half).astype(F32)
        squares[member, 0:8] += jnp.sum(
            (wide * wide).reshape(slab // 8, 8, half // 128, 128), axis=(0, 2)
        )

    def square_copy(off):
        to = (member + off) % GROUP
        return remote(
            squares.at[member],
            squares.at[member],
            sq_send.at[off],
            sq_recv.at[off],
            blk=group * GROUP + to,
        )

    for off in range(1, GROUP):
        square_copy(off).start()

    loads[1].wait()

    @pl.loop(0, tiles)
    def _(step):
        gram = jnp.zeros((slab, tile), F32)
        for part in (0, 1):
            gram = gram + lax.dot_general(
                gbuf[part, my_quad, member // 4].reshape(slab, half),
                gbuf[part, step].reshape(tile, half),
                (((1,), (1,)), ((), ())),
                preferred_element_type=F32,
            )
        for side in range(2):
            natural = side * 4 + (step + quarter) % 4
            cols = pl.ds(pl.multiple_of(natural * 128, 128), 128)
            lstat[:, cols] = (
                STAT_DECAY * lstat[:, cols]
                + (1.0 - STAT_DECAY) * gram[:, side * 128 : (side + 1) * 128]
            )

    store_left = pltpu.make_async_copy(lstat, newl_ref, out_sem.at[0])
    store_left.start()

    for off in range(1, GROUP):
        square_copy(off).wait_recv()
    total = jnp.sum(squares[...], axis=0)
    grad_square = jnp.sum(total[0:8], keepdims=True)
    update_square = jnp.sum(total[8:16], keepdims=True)
    scale = jnp.sqrt((grad_square + GRAFT_EPS) / (update_square + GRAFT_EPS))
    scales[group] = jnp.broadcast_to(scale, (8, 128))

    def scale_copy(off):
        to = (group + off) % groups
        return remote(
            scales.at[group],
            scales.at[group],
            sc_send.at[off],
            sc_recv.at[off],
            blk=to * GROUP + member,
        )

    for off in range(1, groups):
        scale_copy(off).start()

    loads[2].wait()
    first = pl.ds(pl.multiple_of(member % 4 * slab, slab), slab)
    columns = gbuf[member // 4, :, :, :, :, :, first].reshape(width, slab).T

    for part in (0, 1):

        @pl.loop(0, half // tile)
        def _(step):
            cols = pl.ds(pl.multiple_of(step * tile, tile), tile)
            to = pl.ds(pl.multiple_of(part * half + step * tile, tile), tile)
            grad = gbuf[part, :, :, :, :, :, cols].reshape(width, tile)
            gram = jnp.dot(columns, grad, preferred_element_type=F32)
            rstat[:, to] = STAT_DECAY * rstat[:, to] + (1.0 - STAT_DECAY) * gram

    store_right = pltpu.make_async_copy(rstat, newr_ref, out_sem.at[1])
    store_right.start()

    for part in (0, 1):
        for off in range(1, replicas):
            reduce_copy(part, off).wait_send()
        for across, ahead in spread_order:
            spread_copy(part, across, ahead).wait_send()
        for step in range(10):
            handed_on(part, step)
        for quad in range(4):
            cross_quad(part, quad).wait_send()
    qgather.drain()
    root_swap.wait_send()
    factor_swap.wait_send()
    for off in range(1, GROUP):
        square_copy(off).wait_send()
    for off in range(1, groups):
        scale_copy(off).wait_send()
        scale_copy(off).wait_recv()

    pltpu.make_async_copy(uland, uland, up_recv).wait()
    for block in range(groups):
        factor = scales[block, 0:1]
        for part in range(GROUP):
            piece = uland[block, part // 2, :, part % 2 * slab : (part % 2 + 1) * slab]
            ubuf[block, :, part * slab : (part + 1) * slab] = (
                piece.astype(F32) * factor
            ).astype(BF16)
    store_update = pltpu.make_async_copy(ubuf, update_ref, out_sem.at[2])
    store_update.start()
    others = usend.at[pl.ds(0, ends - 1)]
    pl.when(xl == core)(lambda: pltpu.make_async_copy(others, others, up_send).wait())
    pl.when(xl != core)(lambda: pltpu.make_async_copy(usend, usend, up_send).wait())
    store_left.wait()
    store_right.wait()
    store_update.wait()


def on_device(replicas, owners, gradients, left_stat, right_stat, left_root, right_root):
    _, row_count, block_count, width = gradients.shape
    local = block_count // replicas
    slab = width // GROUP
    part = width // owners
    groups = owners // GROUP
    half = width // 2
    dma = pltpu.SemaphoreType.DMA
    update, new_left, new_right = pl.pallas_call(
        functools.partial(kernel, replicas, owners),
        out_shape=(
            jax.ShapeDtypeStruct((local, part, width), BF16),
            jax.ShapeDtypeStruct((slab, width), F32),
            jax.ShapeDtypeStruct((slab, width), F32),
        ),
        in_specs=[pl.BlockSpec(memory_space=pltpu.HBM)] * 5,
        out_specs=[pl.BlockSpec(memory_space=pl.ANY)] * 3,
        scratch_shapes=[
            pltpu.VMEM((2, replicas, row_count, local, half), BF16),
            pltpu.VMEM((half // 128, row_count * local, 128), F32),
            pltpu.VMEM((2, local, row_count, half), BF16),
            pltpu.VMEM((2, 4, 2, 4, 2, row_count, half), BF16),
            pltpu.VMEM((4, 2 * slab, width // 2), BF16),
            pltpu.VMEM((2 * slab, width), BF16),
            pltpu.VMEM((slab, width), F32),
            pltpu.VMEM((slab, width), F32),
            pltpu.VMEM((2 * slab, width), BF16),
            pltpu.VMEM((owners // 2, part, 2 * slab), BF16),
            pltpu.VMEM((groups, 4, part, 2 * slab), BF16),
            pltpu.VMEM((GROUP, 16, 128), F32),
            pltpu.VMEM((groups, 8, 128), F32),
            pltpu.VMEM((local, part, width), BF16),
            dma((3,)),
            dma((2,)),
            dma((GROUP,)),
            dma((2, replicas)),
            dma((2, replicas)),
            dma((2,)),
            dma((2,)),
            dma((4, 2)),
            dma((4,)),
            dma((2, 2, 4)),
            dma((2, 2, 16)),
            dma((2, 16)),
            dma((2, 4)),
            dma((2, 4)),
            dma((GROUP,)),
            dma((GROUP,)),
            dma((groups,)),
            dma((groups,)),
            dma,
            dma,
            dma((3,)),
        ],
        compiler_params=pltpu.CompilerParams(
            collective_id=0, has_side_effects=True, vmem_limit_bytes=40 * 2**20
        ),
        cost_estimate=pl.CostEstimate(
            flops=8 * slab * width * width, bytes_accessed=8 * 2**20, transcendentals=0
        ),
    )(
        *(
            pltpu.with_memory_space_constraint(x, pltpu.HBM)
            for x in (
                gradients.reshape(row_count, replicas, local, width),
                left_stat[0],
                right_stat[0],
                left_root[0],
                right_root[0],
            )
        )
    )
    return jnp.swapaxes(update, 1, 2), new_left[None], new_right[None]


def solution(mesh):
    specs = (P("dp", "blk", None, None),) + (P(("dp", "blk"), None, None),) * 4
    out_specs = (P("dp", None, "blk"), P(("dp", "blk"), None, None), P(("dp", "blk"), None, None))
    return jax.shard_map(
        functools.partial(on_device, mesh.shape["dp"], mesh.shape["blk"]),
        mesh=mesh,
        in_specs=specs,
        out_specs=out_specs,
        check_vma=False,
    )
```

time: 106 us -> 112 us (1.057)
  Pallas kernels: 103 us -> 109 us
    pallas_call x1, Pallas kernels: 103 us -> 109 us  [on_device(): pl.pallas_call(functools.partial(kernel, replicas, owners), out_shape=(ja...]
where the time goes in v6:
time: 112 us
  Pallas kernels  109 us (97%)
  local copies, waits for them, and re-layouts  2.29 us (2%)
    pallas_call x1, Pallas kernels, on_device(): pl.pallas_call(functools.partial(kernel, replicas, owners), out_shape=(ja...  109 us
    unnamed x3, local copies, waits for them, and re-layouts  2.29 us

profile of v6, /device:TPU:1, one launch (start us, length us, event | category | flops | bytes accessed | tf_op | source)
XLA Modules:
  0.0 112.2 jit_solution(11425960257299336760)
XLA Ops:
  0.6 109.3 %shard_map.76 = (bf16[8,16,1024]{2,1,0:T(8,128)(2,1)S(1)}, f32[128,1024]{1,0:T(8,128)S(1)}, f32[128,1024]{1,0:T(8,128)S(1)}) custom-call(bf16[16,8,8,1024]{3,2,1,0:T(8,128)(2,1)} %bitcast.11, f32[128,1024]{1,0:T(8,128)} %bitcast.12, f32[128,1024]{1,0:T(8,128)} %bitcast.13, bf16[128,1024]{1,0:T(8,128)(2,1)} %bitcast.14, bf16[128,1024]{1,0:T(8,128)(2,1)} %bitcast.15), custom_call_target="tpu_custom_call" | custom-call | flops 1073741824 | bytes 8388608 | tf_op jit(solution)/shard_map/pallas_call | solution.py:518
  109.9 0.7 copy.11
  110.7 0.8 copy.12
  111.4 0.8 copy.13

commit v7 on v5

--- a/solution.py
+++ b/solution.py
@@ -217,9 +217,11 @@
         return remote(src, dst, x_send.at[stage, route], x_recv.at[stage, route], **where)
 
     ways = (0, 1)
-    for which in (0, 1):
-        for way in ways:
-            y_copy(0, way, which).start()
+    for way in ways:
+        y_copy(0, way, 0).start()
+    for way in ways:
+        y_copy(1, way, 0).start()
+        y_copy(0, way, 1).start()
 
     root_swap = remote(
         rroot_ref.at[:, half_of(1 - core)],
@@ -260,9 +262,10 @@
         y_add(way, 0)
         y_copy(2, way, 0).start()
     for way in ways:
-        y_copy(1, way, 0).start()
+        y_copy(1, way, 1).start()
     for way in ways:
         y_add(way, 1)
+        y_copy(2, way, 1).start()
 
     def y_total(part, which, row):
         return (
@@ -280,9 +283,6 @@
             xout[part, row] = y_total(part, 0, row).astype(BF16)
 
         x_copy(0, part).start()
-    for kind in (2, 1):
-        for way in ways:
-            y_copy(kind, way, 1).start()
     qgather.hop(1)
     for route in ways:
         x_copy(0, route).wait_recv()
@@ -330,20 +330,10 @@
     def slot_view(slot, which=core):
         return gbuf.at[slot // 4, :, slot % 4, which]
 
-    reach = {1: 4 - chip, 3: chip + 1, 2: jnp.where((chip == 1) | (chip == 2), 6, 5)}
-
-    def spread_to(distance, action):
-        for ahead, lowest, highest in ((1, 1, 4), (3, 1, 4), (2, 5, 6)):
-            if lowest <= distance <= highest:
-
-                @pl.when(reach[ahead] == distance)
-                def _():
-                    for across in (0, 1):
-                        action(spread_copy(across, ahead))
-
-    spread_copy(1, 0).start()
-    spread_to(1, lambda copy: copy.start())
-    spread_to(2, lambda copy: copy.start())
+    spreads = [spread_copy(1, 0)]
+    spreads += [spread_copy(across, ahead) for ahead in (2, 1, 3) for across in (1, 0)]
+    for spread in spreads:
+        spread.start()
     own_slot = gbuf.at[0, xl, chip, core]
     pltpu.make_async_copy(summed.at[group], own_slot, gg_recv.at[chip]).start()
 
@@ -410,8 +400,6 @@
                 lacc[:, cols] = part
 
     def compute(step):
-        if step <= 4:
-            spread_to(step + 2, lambda copy: copy.start())
         if step == 3:
             cross_quad(0).start()
         elif step == 5:
@@ -544,9 +532,8 @@
     qgather.drain()
     root_swap.wait_send()
     factor_swap.wait_send()
-    spread_copy(1, 0).wait_send()
-    for distance in range(1, 7):
-        spread_to(distance, lambda copy: copy.wait_send())
+    for spread in spreads:
+        spread.wait_send()
     pl.when(chip < 3)(lambda: pass_copy(chip, 0).wait_send())
     pl.when(chip > 0)(lambda: pass_copy(chip, 1).wait_send())
     passing(sent)

time: 106 us -> 105 us (level)
  no operation moved by 1% of the time
where the time goes in v7:
time: 105 us
  Pallas kernels  102 us (97%)
  local copies, waits for them, and re-layouts  2.29 us (2%)
    pallas_call x1, Pallas kernels, on_device(): pl.pallas_call(functools.partial(kernel, replicas, owners), out_shape=(ja...  102 us
    unnamed x3, local copies, waits for them, and re-layouts  2.29 us

profile of v7, /device:TPU:1, one launch (start us, length us, event | category | flops | bytes accessed | tf_op | source)
XLA Modules:
  0.0 105.2 jit_solution(3423339596333342434)
XLA Ops:
  0.6 102.3 %shard_map.76 = (bf16[8,16,1024]{2,1,0:T(8,128)(2,1)S(1)}, f32[128,1024]{1,0:T(8,128)S(1)}, f32[128,1024]{1,0:T(8,128)S(1)}) custom-call(bf16[16,8,8,1024]{3,2,1,0:T(8,128)(2,1)} %bitcast.11, f32[128,1024]{1,0:T(8,128)} %bitcast.12, f32[128,1024]{1,0:T(8,128)} %bitcast.13, bf16[128,1024]{1,0:T(8,128)(2,1)} %bitcast.14, bf16[128,1024]{1,0:T(8,128)(2,1)} %bitcast.15), custom_call_target="tpu_custom_call" | custom-call | flops 1073741824 | bytes 8388608 | tf_op jit(solution)/shard_map/pallas_call | solution.py:575
  102.9 0.7 copy.11
  103.6 0.8 copy.12
  104.4 0.8 copy.13

commit v8 on v7

--- a/solution.py
+++ b/solution.py
@@ -66,6 +66,74 @@
             left, right = chip - hop, chip + hop
             pl.when((left >= 0) & (chip < 3))(lambda: self.copy(left, 0).wait_send())
             pl.when((right <= 3) & (chip > 0))(lambda: self.copy(right, 1).wait_send())
+
+
+class GroupGather:
+    def __init__(self, view, group, member, send, recv):
+        self.view, self.group, self.member = view, group, member
+        self.send, self.recv = send, recv
+        self.chip, self.core = member // 2, member % 2
+
+    def copy(self, slot, target, way):
+        return remote(
+            self.view(slot),
+            self.view(slot),
+            self.send.at[slot, way],
+            self.recv.at[slot],
+            blk=self.group * GROUP + target,
+        )
+
+    def to_right(self, slot):
+        return self.copy(slot, self.member + 2, 0)
+
+    def to_left(self, slot):
+        return self.copy(slot, self.member - 2, 1)
+
+    def to_sibling(self, slot):
+        return self.copy(slot, self.chip * 2 + 1 - self.core, 2)
+
+    def own(self):
+        slot = self.member
+        pl.when(self.chip < 3)(lambda: self.to_right(slot).start())
+        pl.when(self.chip > 0)(lambda: self.to_left(slot).start())
+        self.to_sibling(slot).start()
+
+    def hop(self, hop):
+        left, right = self.member - 2 * hop, self.member + 2 * hop
+
+        @pl.when(self.chip >= hop)
+        def _():
+            self.to_right(left).wait_recv()
+            pl.when(self.chip < 3)(lambda: self.to_right(left).start())
+            self.to_sibling(left).start()
+
+        @pl.when(self.chip + hop <= 3)
+        def _():
+            self.to_left(right).wait_recv()
+            pl.when(self.chip > 0)(lambda: self.to_left(right).start())
+            self.to_sibling(right).start()
+
+    def finish(self):
+        for other in range(4):
+            self.to_sibling(other * 2 + 1 - self.core).wait_recv()
+
+    def drain(self):
+        chip = self.chip
+        pl.when(chip < 3)(lambda: self.to_right(self.member).wait_send())
+        pl.when(chip > 0)(lambda: self.to_left(self.member).wait_send())
+        self.to_sibling(self.member).wait_send()
+        for hop in range(1, 4):
+            left, right = self.member - 2 * hop, self.member + 2 * hop
+
+            @pl.when(chip >= hop)
+            def _():
+                pl.when(chip < 3)(lambda: self.to_right(left).wait_send())
+                self.to_sibling(left).wait_send()
+
+            @pl.when(chip + hop <= 3)
+            def _():
+                pl.when(chip > 0)(lambda: self.to_left(right).wait_send())
+                self.to_sibling(right).wait_send()
 
 
 def kernel(
@@ -112,10 +180,9 @@
     qg_send,
     qg_recv,
     sp_send,
+    sp_recv,
     gg_send,
     gg_recv,
-    sib_send,
-    sib_recv,
     sq_send,
     sq_recv,
     sc_send,
@@ -155,7 +222,7 @@
         pltpu.make_async_copy(right_ref, rstat, local_sem.at[3]),
     ]
     for block in range(GROUP):
-        natural = (block % 2) * 4 + (block // 2 + quarter) % 4
+        natural = (block % 2) * 4 + (quarter - block // 2 + 4) % 4
         loads.append(
             pltpu.make_async_copy(
                 lroot_ref.at[:, pl.ds(pl.multiple_of(natural * 128, 128), 128)],
@@ -308,112 +375,58 @@
             ].astype(BF16)
 
     def spread_copy(across, ahead):
-        to_quarter = (quarter + ahead) % 4
-        to_xl = (xl + across) % 2
-        slot = (chip - 4 * ahead) % 16
-        if ahead == 0:
-            entry = chip
-        elif ahead == 1:
-            entry = 0
-        elif ahead == 3:
-            entry = 3
-        else:
-            entry = jnp.where(chip <= 1, 3, 0)
+        to = (xl + across) % 2 * 4 + (quarter + ahead) % 4
         return remote(
-            summed.at[to_xl * 4 + to_quarter],
-            gbuf.at[slot // 4, xl, slot % 4, core],
+            summed.at[to],
+            gbuf.at[ahead, xl, chip, core],
             sp_send.at[across, ahead],
-            gg_recv.at[slot],
-            blk=((to_xl * 4 + to_quarter) * 4 + entry) * 2 + core,
-        )
-
-    def slot_view(slot, which=core):
-        return gbuf.at[slot // 4, :, slot % 4, which]
+            sp_recv.at[ahead // 2],
+            blk=to * GROUP + member,
+        )
 
     spreads = [spread_copy(1, 0)]
-    spreads += [spread_copy(across, ahead) for ahead in (2, 1, 3) for across in (1, 0)]
+    spreads += [spread_copy(across, ahead) for ahead in (1, 3, 2) for across in (1, 0)]
     for spread in spreads:
         spread.start()
     own_slot = gbuf.at[0, xl, chip, core]
-    pltpu.make_async_copy(summed.at[group], own_slot, gg_recv.at[chip]).start()
-
-    def pass_copy(slot, way):
-        view = slot_view(slot)
-        target = member + 2 if way == 0 else member - 2
-        return remote(
-            view, view, gg_send.at[way, slot], gg_recv.at[slot], blk=group * GROUP + target
-        )
-
-    def cross_slot(slot):
-        view = slot_view(slot)
-        return remote(view, view, sib_send.at[slot], sib_recv.at[slot], blk=sibling)
-
-    def cross_quad(quad):
-        view = gbuf.at[quad, :, :, core]
-        return remote(view, view, sib_send.at[quad], sib_recv.at[quad], blk=sibling)
-
-    def wait_slot(slot):
-        view = slot_view(slot)
-        pltpu.make_async_copy(view, view, gg_recv.at[slot]).wait()
-
-    wait_slot(chip)
-    pl.when(chip < 3)(lambda: pass_copy(chip, 0).start())
-    pl.when(chip > 0)(lambda: pass_copy(chip, 1).start())
-
-    def passing(action, between=None):
-        for step in range(1, 10):
-            from_left = (chip - step + 16) % 16
-            from_right = chip + step
-            pl.when(step <= chip + 6)(functools.partial(action, from_left, 0, chip < 3))
-            pl.when(step <= 9 - chip)(functools.partial(action, from_right, 1, chip > 0))
-            if between is not None:
-                between(step)
-
-    def forward(slot, way, more):
-        wait_slot(slot)
-        pl.when(more)(lambda: pass_copy(slot, way).start())
-        pl.when(slot // 4 == 2)(lambda: cross_slot(slot).start())
-
-    def sent(slot, way, more):
-        pl.when(more)(lambda: pass_copy(slot, way).wait_send())
-
-    def apply_quad(quad, first):
-        if quad == 2:
-            for slot in range(8, 12):
-                view = slot_view(slot, 1 - core)
-                pltpu.make_async_copy(view, view, sib_recv.at[slot]).wait()
-        else:
-            view = gbuf.at[quad, :, :, 1 - core]
-            pltpu.make_async_copy(view, view, sib_recv.at[quad]).wait()
-        factor = proot[:, quad * 256 : (quad + 1) * 256]
+    pltpu.make_async_copy(summed.at[group], own_slot, sp_recv.at[0]).start()
+
+    def part_view(part, slot):
+        return gbuf.at[pl.ds(2 * part, 2), :, slot // 2, slot % 2]
+
+    gathers = [
+        GroupGather(
+            functools.partial(part_view, part),
+            group,
+            member,
+            gg_send.at[part],
+            gg_recv.at[part],
+        )
+        for part in (0, 1)
+    ]
+    for part in (0, 1):
+        view = part_view(part, member)
+        pltpu.make_async_copy(view, view, sp_recv.at[part]).wait()
+        gathers[part].own()
+    for hop in (1, 2, 3):
+        for part in (0, 1):
+            gathers[part].hop(hop)
+
+    factor_swap.wait_recv()
+    for part in (0, 1):
+        gathers[part].finish()
+        factor = proot[:, part * 512 : (part + 1) * 512]
 
         @pl.loop(0, tiles)
         def _(step):
             cols = pl.ds(pl.multiple_of(step * tile, tile), tile)
-            grad = gbuf[quad, :, :, :, :, cols].reshape(256, tile)
-            part = jnp.dot(factor, grad, preferred_element_type=F32)
-            if not first:
-                part = part + lacc[:, cols]
-            if quad == 2:
-                lapp[:, cols] = part.astype(BF16)
+            grad = gbuf[2 * part : 2 * part + 2, :, :, :, :, cols].reshape(512, tile)
+            product = jnp.dot(factor, grad, preferred_element_type=F32)
+            if part == 0:
+                lacc[:, cols] = product
             else:
-                lacc[:, cols] = part
-
-    def compute(step):
-        if step == 3:
-            cross_quad(0).start()
-        elif step == 5:
-            factor_swap.wait_recv()
-            apply_quad(0, True)
-        elif step == 7:
-            cross_quad(1).start()
-            cross_quad(3).start()
-        elif step == 9:
-            apply_quad(1, False)
-            apply_quad(3, False)
-
-    passing(forward, compute)
-    apply_quad(2, False)
+                lapp[:, cols] = (product + lacc[:, cols]).astype(BF16)
+
     qgather.hop(3)
 
     applied = lapp[...]
@@ -448,7 +461,7 @@
         def _(off):
             update_copy(number * per_tile + (b + off) % per_tile).start()
 
-    my_quad = (member % 4 - quarter + 4) % 4
+    my_quad = (quarter - member % 4 + 4) % 4
     rows = gbuf[my_quad, member // 4].reshape(slab, width)
     wide = rows.astype(F32)
     squares[member, 0:8] = jnp.sum(
@@ -477,7 +490,7 @@
             rows, other, (((1,), (1,)), ((), ())), preferred_element_type=F32
         )
         for side in range(2):
-            natural = side * 4 + (step + quarter) % 4
+            natural = side * 4 + (quarter - step + 4) % 4
             cols = pl.ds(pl.multiple_of(natural * 128, 128), 128)
             lstat[:, cols] = (
                 STAT_DECAY * lstat[:, cols]
@@ -534,13 +547,8 @@
     factor_swap.wait_send()
     for spread in spreads:
         spread.wait_send()
-    pl.when(chip < 3)(lambda: pass_copy(chip, 0).wait_send())
-    pl.when(chip > 0)(lambda: pass_copy(chip, 1).wait_send())
-    passing(sent)
-    for quad in (0, 1, 3):
-        cross_quad(quad).wait_send()
-    for slot in range(8, 12):
-        cross_slot(slot).wait_send()
+    for part in (0, 1):
+        gathers[part].drain()
     for off in range(1, GROUP):
         square_copy(off).wait_send()
     for off in range(1, groups):
@@ -610,10 +618,9 @@
             dma((4, 2)),
             dma((4,)),
             dma((2, 4)),
-            dma((2, 16)),
-            dma((16,)),
-            dma((16,)),
-            dma((16,)),
+            dma((2,)),
+            dma((2, GROUP, 3)),
+            dma((2, GROUP)),
             dma((GROUP,)),
             dma((GROUP,)),
             dma((groups,)),

time: 105 us -> 103 us (0.981); the launches traced: 105 us -> 101 us
  Pallas kernels: 102 us -> 98.1 us
    pallas_call x1, Pallas kernels: 102 us -> 98.1 us  [on_device(): pl.pallas_call(functools.partial(kernel, replicas, owners), out_shape=(ja...]
where the time goes in v8:
time: 103 us; the launch traced here: 101 us
  Pallas kernels  98.1 us (95%)
  local copies, waits for them, and re-layouts  2.29 us (2%)
    pallas_call x1, Pallas kernels, on_device(): pl.pallas_call(functools.partial(kernel, replicas, owners), out_shape=(ja...  98.1 us
    unnamed x3, local copies, waits for them, and re-layouts  2.29 us

profile of v8, /device:TPU:1, one launch (start us, length us, event | category | flops | bytes accessed | tf_op | source)
XLA Modules:
  0.0 101.1 jit_solution(1619989263378034916)
XLA Ops:
  0.6 98.1 %shard_map.76 = (bf16[8,16,1024]{2,1,0:T(8,128)(2,1)S(1)}, f32[128,1024]{1,0:T(8,128)S(1)}, f32[128,1024]{1,0:T(8,128)S(1)}) custom-call(bf16[16,8,8,1024]{3,2,1,0:T(8,128)(2,1)} %bitcast.11, f32[128,1024]{1,0:T(8,128)} %bitcast.12, f32[128,1024]{1,0:T(8,128)} %bitcast.13, bf16[128,1024]{1,0:T(8,128)(2,1)} %bitcast.14, bf16[128,1024]{1,0:T(8,128)(2,1)} %bitcast.15), custom_call_target="tpu_custom_call" | custom-call | flops 1073741824 | bytes 8388608 | tf_op jit(solution)/shard_map/pallas_call | solution.py:583
  98.8 0.7 copy.11
  99.5 0.8 copy.12
  100.3 0.8 copy.13

commit v9 on v8

--- a/solution.py
+++ b/solution.py
@@ -242,16 +242,12 @@
         return ((y + step) % 4) * 2 + which
 
     barrier = pltpu.get_barrier_semaphore()
-    for peer in ({"dp": at_y(1, xh)}, {"dp": at_y(3, xh)}, near_b):
-        pl.semaphore_signal(barrier, inc=1, device_id=peer, device_id_type=MESH)
-
-    @pl.loop(1, owners)
-    def _(off):
-        pl.semaphore_signal(
-            barrier, inc=1, device_id={"blk": (b + off) % owners}, device_id_type=MESH
-        )
-
-    pl.semaphore_wait(barrier, 3 + owners - 1)
+    partners = [{"dp": at_y(1, xh)}, {"dp": at_y(3, xh)}, near_b]
+    partners += [{"blk": group * GROUP + (member + off) % GROUP} for off in range(1, GROUP)]
+    partners += [{"blk": (group + off) % groups * GROUP + member} for off in range(1, groups)]
+    for partner in partners:
+        pl.semaphore_signal(barrier, inc=1, device_id=partner, device_id_type=MESH)
+    pl.semaphore_wait(barrier, len(partners))
 
     sides = (1 - xh, xh)
     steps = (1, 3)

time: 103 us -> 100 us (0.971); the launches traced: 101 us -> 100 us
  Pallas kernels: 98.1 us -> 97 us
    pallas_call x1, Pallas kernels: 98.1 us -> 97 us  [on_device(): pl.pallas_call(functools.partial(kernel, replicas, owners), out_shape=(ja...]
where the time goes in v9:
time: 100 us
  Pallas kernels  97 us (97%)
  local copies, waits for them, and re-layouts  2.29 us (2%)
    pallas_call x1, Pallas kernels, on_device(): pl.pallas_call(functools.partial(kernel, replicas, owners), out_shape=(ja...  97 us
    unnamed x3, local copies, waits for them, and re-layouts  2.29 us

profile of v9, /device:TPU:1, one launch (start us, length us, event | category | flops | bytes accessed | tf_op | source)
XLA Modules:
  0.0 100.0 jit_solution(18402238565562095092)
XLA Ops:
  0.6 97.0 %shard_map.76 = (bf16[8,16,1024]{2,1,0:T(8,128)(2,1)S(1)}, f32[128,1024]{1,0:T(8,128)S(1)}, f32[128,1024]{1,0:T(8,128)S(1)}) custom-call(bf16[16,8,8,1024]{3,2,1,0:T(8,128)(2,1)} %bitcast.11, f32[128,1024]{1,0:T(8,128)} %bitcast.12, f32[128,1024]{1,0:T(8,128)} %bitcast.13, bf16[128,1024]{1,0:T(8,128)(2,1)} %bitcast.14, bf16[128,1024]{1,0:T(8,128)(2,1)} %bitcast.15), custom_call_target="tpu_custom_call" | custom-call | flops 1073741824 | bytes 8388608 | tf_op jit(solution)/shard_map/pallas_call | solution.py:579
  97.7 0.7 copy.11
  98.4 0.8 copy.12
  99.2 0.8 copy.13

commit v10 on v9

--- a/solution.py
+++ b/solution.py
@@ -168,7 +168,6 @@
     uland,
     squares,
     scales,
-    ubuf,
     local_sem,
     root_sem,
     y_send,
@@ -284,7 +283,6 @@
         y_copy(0, way, 0).start()
     for way in ways:
         y_copy(1, way, 0).start()
-        y_copy(0, way, 1).start()
 
     root_swap = remote(
         rroot_ref.at[:, half_of(1 - core)],
@@ -324,11 +322,9 @@
     for way in ways:
         y_add(way, 0)
         y_copy(2, way, 0).start()
-    for way in ways:
-        y_copy(1, way, 1).start()
-    for way in ways:
-        y_add(way, 1)
-        y_copy(2, way, 1).start()
+    for kind in (0, 1):
+        for way in ways:
+            y_copy(kind, way, 1).start()
 
     def y_total(part, which, row):
         return (
@@ -346,6 +342,9 @@
             xout[part, row] = y_total(part, 0, row).astype(BF16)
 
         x_copy(0, part).start()
+    for way in ways:
+        y_add(way, 1)
+        y_copy(2, way, 1).start()
     qgather.hop(1)
     for route in ways:
         x_copy(0, route).wait_recv()
@@ -556,17 +555,14 @@
         factor = scales[block, 0:1]
         for part in range(GROUP):
             piece = uland[block, part // 2, :, part % 2 * slab : (part % 2 + 1) * slab]
-            ubuf[block, :, part * slab : (part + 1) * slab] = (
+            update_ref[block, :, part * slab : (part + 1) * slab] = (
                 piece.astype(F32) * factor
             ).astype(BF16)
-    store_update = pltpu.make_async_copy(ubuf, update_ref, out_sem.at[2])
-    store_update.start()
     others = usend.at[pl.ds(0, ends - 1)]
     pl.when(xl == core)(lambda: pltpu.make_async_copy(others, others, up_send).wait())
     pl.when(xl != core)(lambda: pltpu.make_async_copy(usend, usend, up_send).wait())
     store_left.wait()
     store_right.wait()
-    store_update.wait()
 
 
 def on_device(replicas, owners, gradients, left_stat, right_stat, left_root, right_root):
@@ -584,7 +580,7 @@
             jax.ShapeDtypeStruct((slab, width), F32),
         ),
         in_specs=[pl.BlockSpec(memory_space=pltpu.HBM)] * 5,
-        out_specs=[pl.BlockSpec(memory_space=pl.ANY)] * 3,
+        out_specs=[pl.BlockSpec(memory_space=pltpu.VMEM)] + [pl.BlockSpec(memory_space=pl.ANY)] * 2,
         scratch_shapes=[
             pltpu.VMEM((row_count, replicas, local, width), BF16),
             *[pltpu.VMEM((2, 2, row_count // 2, local, width), BF16)] * 4,
@@ -602,7 +598,6 @@
             pltpu.VMEM((groups, 4, part, 2 * slab), BF16),
             pltpu.VMEM((GROUP, 16, 128), F32),
             pltpu.VMEM((groups, 8, 128), F32),
-            pltpu.VMEM((local, part, width), BF16),
             dma((4,)),
             dma((GROUP,)),
             dma((3, 2, 2)),

time: 100 us -> 101 us (1.010)
  no operation moved by 1% of the time
where the time goes in v10:
time: 101 us
  Pallas kernels  97.6 us (97%)
  local copies, waits for them, and re-layouts  2.29 us (2%)
    pallas_call x1, Pallas kernels, on_device(): pl.pallas_call(functools.partial(kernel, replicas, owners), out_shape=(ja...  97.6 us
    unnamed x3, local copies, waits for them, and re-layouts  2.29 us

profile of v10, /device:TPU:1, one launch (start us, length us, event | category | flops | bytes accessed | tf_op | source)
XLA Modules:
  0.0 100.5 jit_solution(5210253205898244987)
XLA Ops:
  0.6 97.6 %shard_map.76 = (bf16[8,16,1024]{2,1,0:T(8,128)(2,1)S(1)}, f32[128,1024]{1,0:T(8,128)S(1)}, f32[128,1024]{1,0:T(8,128)S(1)}) custom-call(bf16[16,8,8,1024]{3,2,1,0:T(8,128)(2,1)} %bitcast.11, f32[128,1024]{1,0:T(8,128)} %bitcast.12, f32[128,1024]{1,0:T(8,128)} %bitcast.13, bf16[128,1024]{1,0:T(8,128)(2,1)} %bitcast.14, bf16[128,1024]{1,0:T(8,128)(2,1)} %bitcast.15), custom_call_target="tpu_custom_call" | custom-call | flops 1073741824 | bytes 8388608 | tf_op jit(solution)/shard_map/pallas_call | solution.py:575
  98.2 0.7 copy.11
  99.0 0.8 copy.12
  99.7 0.8 copy.13

commit v11 on v9

--- a/solution.py
+++ b/solution.py
@@ -294,6 +294,20 @@
         blk=sibling,
     )
     root_swap.start()
+    qgathers = [
+        LineGather(
+            functools.partial(lambda which, s: qbuf.at[s, part_of(which)], which),
+            group * GROUP + core,
+            chip,
+            qg_send.at[piece],
+            qg_recv.at[piece],
+        )
+        for piece, which in ((0, core), (1, 1 - core))
+    ]
+    loads[1].wait()
+    qgathers[0].own()
+    root_swap.wait_recv()
+    qgathers[1].own()
     for load in loads[4:]:
         load.wait()
     factor_swap = remote(
@@ -304,12 +318,6 @@
         blk=sibling,
     )
     factor_swap.start()
-    loads[1].wait()
-    root_swap.wait_recv()
-    qgather = LineGather(
-        lambda s: qbuf.at[s], group * GROUP + core, chip, qg_send, qg_recv
-    )
-    qgather.own()
     loads[0].wait()
 
     def y_add(way, which):
@@ -346,11 +354,13 @@
             xout[part, row] = y_total(part, 0, row).astype(BF16)
 
         x_copy(0, part).start()
-    qgather.hop(1)
+    for qgather in qgathers:
+        qgather.hop(1)
     for route in ways:
         x_copy(0, route).wait_recv()
         x_copy(1, route).start()
-    qgather.hop(2)
+    for qgather in qgathers:
+        qgather.hop(2)
 
     for part in ways:
         y_copy(2, part, 1).wait_recv()
@@ -423,7 +433,8 @@
             else:
                 lapp[:, cols] = (product + lacc[:, cols]).astype(BF16)
 
-    qgather.hop(3)
+    for qgather in qgathers:
+        qgather.hop(3)
 
     applied = lapp[...]
     squares[member] = jnp.zeros((16, 128), F32)
@@ -538,7 +549,8 @@
     for route in ways:
         x_copy(0, route).wait_send()
         x_copy(1, route).wait_send()
-    qgather.drain()
+    for qgather in qgathers:
+        qgather.drain()
     root_swap.wait_send()
     factor_swap.wait_send()
     for spread in spreads:
@@ -611,8 +623,8 @@
             dma((2, 2)),
             dma((2,)),
             dma((2,)),
-            dma((4, 2)),
-            dma((4,)),
+            dma((2, 4, 2)),
+            dma((2, 4)),
             dma((2, 4)),
             dma((2,)),
             dma((2, GROUP, 3)),

time: 100 us -> 100 us (level)
  no operation moved by 1% of the time
where the time goes in v11:
time: 100 us
  Pallas kernels  97.2 us (97%)
  local copies, waits for them, and re-layouts  2.29 us (2%)
    pallas_call x1, Pallas kernels, on_device(): pl.pallas_call(functools.partial(kernel, replicas, owners), out_shape=(ja...  97.2 us
    unnamed x3, local copies, waits for them, and re-layouts  2.29 us

profile of v11, /device:TPU:1, one launch (start us, length us, event | category | flops | bytes accessed | tf_op | source)
XLA Modules:
  0.0 100.2 jit_solution(8460255832021436241)
XLA Ops:
  0.6 97.2 %shard_map.76 = (bf16[8,16,1024]{2,1,0:T(8,128)(2,1)S(1)}, f32[128,1024]{1,0:T(8,128)S(1)}, f32[128,1024]{1,0:T(8,128)S(1)}) custom-call(bf16[16,8,8,1024]{3,2,1,0:T(8,128)(2,1)} %bitcast.11, f32[128,1024]{1,0:T(8,128)} %bitcast.12, f32[128,1024]{1,0:T(8,128)} %bitcast.13, bf16[128,1024]{1,0:T(8,128)(2,1)} %bitcast.14, bf16[128,1024]{1,0:T(8,128)(2,1)} %bitcast.15), custom_call_target="tpu_custom_call" | custom-call | flops 1073741824 | bytes 8388608 | tf_op jit(solution)/shard_map/pallas_call | solution.py:591
  97.9 0.7 copy.11
  98.6 0.8 copy.12
  99.4 0.8 copy.13
